TPU v7x, 256 devices: a whole 4x4x8 slice. The times are simulated.
256 devices in a mesh: section: 2 (over core), expert: 16 (over y, x), dp: 8 (over z).
Axes of the slice: x: 4, y: 4, z: 8, core: 2. Of those that a mesh axis runs over, the one named last changes fastest.
Arguments:
- tokens: bfloat16 [2, 8192, 768], P('section', 'dp', 'expert'), may hold values from -6 to 6
- norm_gain: bfloat16 [2, 768], P('section', 'expert'), may hold values from 0.099609375 to 1.8984375
- w_gate: bfloat16 [2, 768, 12288], P('section', None, 'expert'), may hold values from -0.21875 to 0.21875
- w_up: bfloat16 [2, 768, 12288], P('section', None, 'expert'), may hold values from -0.21875 to 0.21875
- w_down: bfloat16 [2, 12288, 768], P('section', 'expert'), may hold values from -0.75 to 0.75
- expert_ids: int32 [2, 4, 8192, 2], P('section', None, 'dp'), may hold values from 0 to 7, all different within a row; in each aligned block of 1024 rows (0 to 1023, 1024 to 2047, ..., all dimensions but the last counted through in order) at most 512 rows name the same one
- gate_logits: float32 [2, 4, 8192, 2], P('section', None, 'dp'), may hold values from -0.3 to 0.3
Outputs:
- carried: bfloat16 [2, 8192, 768], P('section', 'dp', 'expert')
Inputs may be any that keep to these rules, and one draw needn't show every extreme that they name: `expert_ids`: A row names two different experts. In each block of 1024 rows that one index of dp holds for one section and stop, no expert is named by more than 512 rows, and one is named by exactly 512.
All inputs are finite; a program needn't handle non-finite values.
Results may differ from a plain program's by a relative error of at most 0.019.
Values may be sent and summed in bfloat16 or wider, within the bound.
A program may use at most 64 MiB of HBM per device.

v0:
```python
import jax
import jax.numpy as jnp
from jax import lax
from jax.sharding import PartitionSpec as P

D = 768
STOPS = 4


def passed_along(array, axis, by):
    devices = lax.axis_size(axis)
    return lax.ppermute(array, axis, [(i, (i + by) % devices) for i in range(devices)])


def expert_ffn(rows_in, gate_w, up_w, down_w):
    gate_val = jnp.dot(rows_in, gate_w, preferred_element_type=jnp.float32)
    up_val = jnp.dot(rows_in, up_w, preferred_element_type=jnp.float32)
    hidden = (jax.nn.silu(gate_val) * up_val).astype(jnp.bfloat16)
    return jnp.dot(hidden, down_w, preferred_element_type=jnp.float32).astype(jnp.bfloat16)


def per_device(tokens, norm_gain, w_gate, w_up, w_down, expert_ids, gate_logits):
    device_count = lax.axis_size("expert")
    pair_count = device_count // 2
    carried = tokens[0]
    row_count = carried.shape[0]
    width_local = carried.shape[1]
    gain_row = norm_gain[0]
    gate_w = w_gate[0]
    up_w = w_up[0]
    down_w = w_down[0]
    capacity = min(row_count, 4 * row_count // pair_count)
    pair_rows = 2 * row_count
    triangle = (jnp.arange(pair_rows)[:, None] >= jnp.arange(pair_rows)[None, :]).astype(
        jnp.float32
    )
    slot_range = jnp.arange(pair_count * capacity, dtype=jnp.int32)
    for stop_num in range(STOPS):
        route_ids = expert_ids[0, stop_num]
        logits = gate_logits[0, stop_num]
        flat_ids = route_ids.reshape(-1)
        one_hot = (flat_ids[:, None] == jnp.arange(pair_count, dtype=jnp.int32)[None, :]).astype(
            jnp.float32
        )
        running = jnp.dot(triangle, one_hot, precision=lax.Precision.HIGHEST)
        slot_pos = (jnp.sum(running * one_hot, axis=1) - 1.0).astype(jnp.int32)
        slot_key = flat_ids * capacity + slot_pos
        selector = (slot_range[:, None] == slot_key[None, :]).astype(jnp.bfloat16)
        widened = carried.astype(jnp.float32)
        sum_squares = lax.psum(jnp.sum(widened * widened, axis=1), "expert")
        inverse = lax.rsqrt(sum_squares / D + 1e-05)
        normed = (widened * inverse[:, None] * gain_row.astype(jnp.float32)).astype(jnp.bfloat16)
        doubled = jnp.repeat(normed, 2, axis=0)
        packed = jnp.dot(selector, doubled, preferred_element_type=jnp.float32).astype(jnp.bfloat16)
        packed = packed.reshape(pair_count, 1, capacity, width_local)
        packed = jnp.broadcast_to(packed, (pair_count, 2, capacity, width_local))
        packed = packed.reshape(device_count, capacity, width_local)
        outcome = expert_ffn(
            lax.all_to_all(packed, "expert", split_axis=0, concat_axis=2, tiled=True)[0],
            gate_w,
            up_w,
            down_w,
        )
        returned = lax.all_to_all(outcome[None], "expert", split_axis=2, concat_axis=0, tiled=True)
        halves = returned.astype(jnp.float32).reshape(pair_count, 2, capacity, width_local)
        combined = (halves[:, 0] + halves[:, 1]).reshape(pair_count * capacity, width_local)
        pulled = jnp.take(combined, slot_key, axis=0).reshape(row_count, 2, width_local)
        weight_one = jax.nn.sigmoid(logits[:, 0] - logits[:, 1])
        weight_two = jax.nn.sigmoid(logits[:, 1] - logits[:, 0])
        updated = widened + weight_one[:, None] * pulled[:, 0] + weight_two[:, None] * pulled[:, 1]
        carried = passed_along(updated.astype(jnp.bfloat16), "section", 1)
    return carried[None]


def solution(mesh):
    placed = (
        P("section", "dp", "expert"),
        P("section", "expert"),
        P("section", None, "expert"),
        P("section", None, "expert"),
        P("section", "expert", None),
        P("section", None, "dp", None),
        P("section", None, "dp", None),
    )
    return jax.shard_map(
        per_device,
        mesh=mesh,
        in_specs=placed,
        out_specs=P("section", "dp", "expert"),
        check_vma=False,
    )
```

profile of v0, /device:TPU:1, one launch (start us, length us, event | category | flops | bytes accessed | tf_op | source)
XLA Modules:
  0.0 442.7 jit_solution(18260930423976638445)
XLA Ops:
  4.0 34.3 %psum.28 = f32[1024]{0:T(1024)S(1)} all-reduce(f32[1024]{0:T(1024)S(1)} %fusion.71), channel_id=1, replica_groups=mesh['section'=2,'expert'=16,'dp'=8] {'expert'}, use_global_device_ids=true, to_apply=%region_2.0 | all-reduce | flops 1024 | bytes 8192 | tf_op jit(solution)/shard_map/psum | solution.py:50
  38.8 6.7 %fusion.15 = bf16[4096,48]{0,1:T(8,128)(2,1)S(1)} fusion(bf16[2048,48]{1,0:T(8,128)(2,1)S(1)} %bitcast.239, s32[2048]{0:T(1024)S(1)} %get-tuple-element.13), kind=kOutput, calls=%fused_computation.24 | convolution fusion | flops 813891584 | bytes 598016 | tf_op jit(solution)/shard_map/dot_general | solution.py:54
  46.6 3.8 all-to-all-start
  50.8 9.9 %all-to-all-done = bf16[16,512,48]{1,2,0:T(8,128)(2,1)S(1)} async-done(((bf16[16,512,48]{1,2,0:T(8,128)(2,1)}), bf16[16,512,48]{1,2,0:T(8,128)(2,1)S(1)}, u32[]{:S(2)}, u32[]{:S(2)}) %all-to-all-start) | async-done | bytes 786464 | tf_op jit(solution)/shard_map/all_to_all | solution.py:59
  60.7 2.0 fusion.38
  62.7 3.8 fusion.20
  68.4 5.5 %reduce = bf16[768,512]{1,0:T(8,128)(2,1)S(1)} reduce(bf16[768,1,512]{2,1,0:T(2,128)(2,1)S(1)} %bitcast.204, bf16[]{:T(256)} %broadcast.147), dimensions={1}, to_apply=%bitcast.176.reduce_sub_computation | reduce | bytes 1572866
  73.9 1.5 reshape.209
  75.3 3.8 all-to-all-start.1
  79.2 2.0 fusion.42
  83.1 6.5 %all-to-all-done.1 = bf16[16,2,12288]{2,1,0:T(2,128)(2,1)S(1)} async-done(((bf16[16,2,12288]{2,1,0:T(2,128)(2,1)}), bf16[16,2,12288]{2,1,0:T(2,128)(2,1)S(1)}, u32[]{:S(2)}, u32[]{:S(2)}) %all-to-all-start.1) | async-done | bytes 786464 | tf_op jit(solution)/shard_map/all_to_all | solution.py:64
  90.9 1.9 copy.100
  92.8 1.9 copy.101
  94.7 2.4 add.175
  97.2 7.6 %gather_fusion = f32[2048,48]{1,0:T(8,128)} fusion(f32[4096,48]{1,0:T(8,128)S(1)} %bitcast.200, s32[2048]{0:T(1024)S(1)} %copy-done.19), kind=kCustom, calls=%fused_computation.clone | custom fusion | bytes 794624 | tf_op jit(solution)/shard_map/jit(_take)/gather | solution.py:67
  104.8 1.6 broadcast_select_fusion.3
  107.9 10.3 %collective-permute-start = (bf16[1024,48]{0,1:T(8,128)(2,1)S(1)}, bf16[1024,48]{0,1:T(8,128)(2,1)S(1)}, u32[]{:S(2)}, u32[]{:S(2)}) collective-permute-start(bf16[1024,48]{0,1:T(8,128)(2,1)S(1)} %fusion.75), channel_id=1, source_target_pairs={{0,128},{128,0},{1,129},{129,1},{2,130},{130,2},{3,131},{131,3},{4... | collective-permute-start | bytes 294920 | tf_op jit(solution)/shard_map/ppermute | solution.py:12
  119.2 29.5 %psum.29 = f32[1024]{0:T(1024)S(1)} all-reduce(f32[1024]{0:T(1024)S(1)} %fusion.56), channel_id=1, replica_groups=mesh['section'=2,'expert'=16,'dp'=8] {'expert'}, use_global_device_ids=true, to_apply=%region_5.7 | all-reduce | flops 1024 | bytes 8192 | tf_op jit(solution)/shard_map/psum | solution.py:50
  149.2 6.7 %fusion.14 = bf16[4096,48]{0,1:T(8,128)(2,1)S(1)} fusion(bf16[2048,48]{1,0:T(8,128)(2,1)S(1)} %bitcast.240, s32[2048]{0:T(1024)S(1)} %get-tuple-element.11), kind=kOutput, calls=%fused_computation.23 | convolution fusion | flops 813891584 | bytes 598016 | tf_op jit(solution)/shard_map/dot_general | solution.py:54
  156.0 13.4 %all_to_all.96 = bf16[16,512,48]{1,2,0:T(8,128)(2,1)S(1)} all-to-all(bf16[16,512,48]{1,2,0:T(8,128)(2,1)S(1)} %bitcast.220), channel_id=1, replica_groups=mesh['section'=2,'expert'=16,'dp'=8] {'expert'}, dimensions={0} | all-to-all | bytes 1572864 | tf_op jit(solution)/shard_map/all_to_all | solution.py:59
  169.4 2.0 fusion.36
  171.4 3.8 fusion.21
  176.5 5.5 %reduce.1 = bf16[768,512]{1,0:T(8,128)(2,1)S(1)} reduce(bf16[768,1,512]{2,1,0:T(2,128)(2,1)S(1)} %bitcast.211, bf16[]{:T(256)} %broadcast.147), dimensions={1}, to_apply=%bitcast.178.reduce_sub_computation | reduce | bytes 1572866
  182.0 1.5 reshape.211
  183.5 3.8 all-to-all-start.3
  187.8 2.0 fusion.41
  190.4 7.2 %all-to-all-done.3 = bf16[16,2,12288]{2,1,0:T(2,128)(2,1)S(1)} async-done(((bf16[16,2,12288]{2,1,0:T(2,128)(2,1)}), bf16[16,2,12288]{2,1,0:T(2,128)(2,1)S(1)}, u32[]{:S(2)}, u32[]{:S(2)}) %all-to-all-start.3) | async-done | bytes 786464 | tf_op jit(solution)/shard_map/all_to_all | solution.py:64
  199.0 1.9 copy.104
  200.9 1.9 copy.105
  202.8 2.4 add.184
  205.3 7.6 %gather_fusion.1 = f32[2048,48]{1,0:T(8,128)} fusion(f32[4096,48]{1,0:T(8,128)S(1)} %bitcast.201, s32[2048]{0:T(1024)S(1)} %copy-done.20), kind=kCustom, calls=%fused_computation.1.clone | custom fusion | bytes 794624 | tf_op jit(solution)/shard_map/jit(_take)/gather | solution.py:67
  212.9 1.6 broadcast_select_fusion.2
  216.0 9.9 %collective-permute-start.1 = (bf16[1024,48]{0,1:T(8,128)(2,1)S(1)}, bf16[1024,48]{0,1:T(8,128)(2,1)S(1)}, u32[]{:S(2)}, u32[]{:S(2)}) collective-permute-start(bf16[1024,48]{0,1:T(8,128)(2,1)S(1)} %fusion.60), channel_id=1, source_target_pairs={{0,128},{128,0},{1,129},{129,1},{2,130},{130,2},{3,131},{131,3},{4... | collective-permute-start | bytes 294920 | tf_op jit(solution)/shard_map/ppermute | solution.py:12
  226.9 29.5 %psum.30 = f32[1024]{0:T(1024)S(1)} all-reduce(f32[1024]{0:T(1024)S(1)} %fusion.61), channel_id=1, replica_groups=mesh['section'=2,'expert'=16,'dp'=8] {'expert'}, use_global_device_ids=true, to_apply=%region_8.10 | all-reduce | flops 1024 | bytes 8192 | tf_op jit(solution)/shard_map/psum | solution.py:50
  257.0 6.7 %fusion.13 = bf16[4096,48]{0,1:T(8,128)(2,1)S(1)} fusion(bf16[2048,48]{1,0:T(8,128)(2,1)S(1)} %bitcast.241, s32[2048]{0:T(1024)S(1)} %get-tuple-element.9), kind=kOutput, calls=%fused_computation.22 | convolution fusion | flops 813891584 | bytes 598016 | tf_op jit(solution)/shard_map/dot_general | solution.py:54
  263.8 13.2 %all_to_all.97 = bf16[16,512,48]{1,2,0:T(8,128)(2,1)S(1)} all-to-all(bf16[16,512,48]{1,2,0:T(8,128)(2,1)S(1)} %bitcast.221), channel_id=1, replica_groups=mesh['section'=2,'expert'=16,'dp'=8] {'expert'}, dimensions={0} | all-to-all | bytes 1572864 | tf_op jit(solution)/shard_map/all_to_all | solution.py:59
  277.0 2.0 fusion.34
  279.0 3.8 fusion.22
  284.1 5.5 %reduce.2 = bf16[768,512]{1,0:T(8,128)(2,1)S(1)} reduce(bf16[768,1,512]{2,1,0:T(2,128)(2,1)S(1)} %bitcast.213, bf16[]{:T(256)} %broadcast.147), dimensions={1}, to_apply=%bitcast.180.reduce_sub_computation | reduce | bytes 1572866
  289.5 1.5 reshape.213
  291.0 4.0 all-to-all-start.5
  295.5 2.0 fusion.40
  298.2 7.2 %all-to-all-done.5 = bf16[16,2,12288]{2,1,0:T(2,128)(2,1)S(1)} async-done(((bf16[16,2,12288]{2,1,0:T(2,128)(2,1)}), bf16[16,2,12288]{2,1,0:T(2,128)(2,1)S(1)}, u32[]{:S(2)}, u32[]{:S(2)}) %all-to-all-start.5) | async-done | bytes 786464 | tf_op jit(solution)/shard_map/all_to_all | solution.py:64
  306.7 1.9 copy.108
  308.7 1.9 copy.109
  310.6 2.4 add.193
  313.0 7.6 %gather_fusion.2 = f32[2048,48]{1,0:T(8,128)} fusion(f32[4096,48]{1,0:T(8,128)S(1)} %bitcast.202, s32[2048]{0:T(1024)S(1)} %fusion.82), kind=kCustom, calls=%fused_computation.2.clone | custom fusion | bytes 794624 | tf_op jit(solution)/shard_map/jit(_take)/gather | solution.py:67
  320.6 1.6 broadcast_select_fusion.1
  323.7 9.9 %collective-permute-start.2 = (bf16[1024,48]{0,1:T(8,128)(2,1)S(1)}, bf16[1024,48]{0,1:T(8,128)(2,1)S(1)}, u32[]{:S(2)}, u32[]{:S(2)}) collective-permute-start(bf16[1024,48]{0,1:T(8,128)(2,1)S(1)} %fusion.65), channel_id=1, source_target_pairs={{0,128},{128,0},{1,129},{129,1},{2,130},{130,2},{3,131},{131,3},{4... | collective-permute-start | bytes 294920 | tf_op jit(solution)/shard_map/ppermute | solution.py:12
  334.6 29.5 %psum.31 = f32[1024]{0:T(1024)S(1)} all-reduce(f32[1024]{0:T(1024)S(1)} %fusion.66), channel_id=1, replica_groups=mesh['section'=2,'expert'=16,'dp'=8] {'expert'}, use_global_device_ids=true, to_apply=%region_11.13 | all-reduce | flops 1024 | bytes 8192 | tf_op jit(solution)/shard_map/psum | solution.py:50
  364.7 6.7 %fusion.12 = bf16[4096,48]{0,1:T(8,128)(2,1)S(1)} fusion(bf16[2048,48]{1,0:T(8,128)(2,1)S(1)} %bitcast.242, s32[2048]{0:T(1024)S(1)} %get-tuple-element.7), kind=kOutput, calls=%fused_computation.21 | convolution fusion | flops 813891584 | bytes 598016 | tf_op jit(solution)/shard_map/dot_general | solution.py:54
  371.5 13.2 %all_to_all.98 = bf16[16,512,48]{1,2,0:T(8,128)(2,1)S(1)} all-to-all(bf16[16,512,48]{1,2,0:T(8,128)(2,1)S(1)} %bitcast.222), channel_id=1, replica_groups=mesh['section'=2,'expert'=16,'dp'=8] {'expert'}, dimensions={0} | all-to-all | bytes 1572864 | tf_op jit(solution)/shard_map/all_to_all | solution.py:59
  384.7 2.0 fusion.32
  386.6 3.8 fusion.23
  391.7 5.5 %reduce.3 = bf16[768,512]{1,0:T(8,128)(2,1)S(1)} reduce(bf16[768,1,512]{2,1,0:T(2,128)(2,1)S(1)} %bitcast.209, bf16[]{:T(256)} %broadcast.147), dimensions={1}, to_apply=%bitcast.182.reduce_sub_computation | reduce | bytes 1572866
  397.2 1.5 reshape.215
  398.7 3.6 all-to-all-start.7
  402.3 10.4 %all-to-all-done.7 = bf16[16,2,12288]{2,1,0:T(2,128)(2,1)S(1)} async-done(((bf16[16,2,12288]{2,1,0:T(2,128)(2,1)}), bf16[16,2,12288]{2,1,0:T(2,128)(2,1)S(1)}, u32[]{:S(2)}, u32[]{:S(2)}) %all-to-all-start.7) | async-done | bytes 786464 | tf_op jit(solution)/shard_map/all_to_all | solution.py:64
  414.0 1.9 copy.112
  416.0 1.9 copy.113
  417.9 2.4 add.202
  420.3 7.6 %gather_fusion.3 = f32[2048,48]{1,0:T(8,128)} fusion(f32[4096,48]{1,0:T(8,128)S(1)} %bitcast.203, s32[2048]{0:T(1024)S(1)} %fusion.83), kind=kCustom, calls=%fused_computation.3.clone | custom fusion | bytes 794624 | tf_op jit(solution)/shard_map/jit(_take)/gather | solution.py:67
  427.9 1.6 broadcast_select_fusion
  431.0 9.9 %collective-permute-start.3 = (bf16[1024,48]{0,1:T(8,128)(2,1)S(1)}, bf16[1024,48]{0,1:T(8,128)(2,1)S(1)}, u32[]{:S(2)}, u32[]{:S(2)}) collective-permute-start(bf16[1024,48]{0,1:T(8,128)(2,1)S(1)} %fusion.70), channel_id=1, source_target_pairs={{0,128},{128,0},{1,129},{129,1},{2,130},{130,2},{3,131},{131,3},{4... | collective-permute-start | bytes 294920 | tf_op jit(solution)/shard_map/ppermute | solution.py:12
  (174 shorter events, 33.5 us)
Async XLA Ops:
  0.0 60.7 %copy-start = (bf16[1,768,768]{2,1,0:T(8,128)(2,1)S(1)}, bf16[1,768,768]{2,1,0:T(8,128)(2,1)}, u32[]{:S(2)}) copy-start(bf16[1,768,768]{2,1,0:T(8,128)(2,1)} %param.11) | copy-start | bytes 3538948
  1.9 2.0 copy-start.40
  2.0 2.0 copy-start.1
  4.0 41.6 %copy-start.11 = (s32[2048]{0:T(1024)}, s32[2048]{0:T(1024)S(1)}, u32[]{:S(2)}) copy-start(s32[2048]{0:T(1024)S(1)} %get-tuple-element.13) | copy-start | bytes 24580
  4.0 34.3 %copy-start.29 = (f32[48]{0:T(128)}, f32[48]{0:T(128)S(1)}, u32[]{:S(2)}) copy-start(f32[48]{0:T(128)S(1)} %bitcast_convert_fusion) | copy-start | bytes 580
  46.6 14.2 %all-to-all-start = ((bf16[16,512,48]{1,2,0:T(8,128)(2,1)}), bf16[16,512,48]{1,2,0:T(8,128)(2,1)S(1)}, u32[]{:S(2)}, u32[]{:S(2)}) async-start(bf16[16,512,48]{1,2,0:T(8,128)(2,1)} %bitcast.6), calls=%async_computation | async-start | bytes 1572864 | tf_op jit(solution)/shard_map/all_to_all | solution.py:59
  75.3 14.2 %all-to-all-start.1 = ((bf16[16,2,12288]{2,1,0:T(2,128)(2,1)}), bf16[16,2,12288]{2,1,0:T(2,128)(2,1)S(1)}, u32[]{:S(2)}, u32[]{:S(2)}) async-start(bf16[16,2,12288]{2,1,0:T(2,128)(2,1)} %reshape.209), calls=%async_computation.1 | async-start | bytes 1572864 | tf_op jit(solution)/shard_map/all_to_all | solution.py:64
  79.1 2.1 copy-start.12
  79.2 2.6 copy-start.10
  94.7 2.5 copy-start.19
  97.2 7.6 %copy-start.33 = (pred[2048]{0:T(1024)(128)(4,1)S(1)}, pred[2048]{0:T(1024)(128)(4,1)}, u32[]{:S(2)}) copy-start(pred[2048]{0:T(1024)(128)(4,1)} %get-tuple-element.12) | copy-start | bytes 6148
  106.4 1.5 copy-start.2
  106.4 1.5 copy-start.27
  106.4 1.5 copy-start.28
  106.4 11.8 %copy-start.37 = (f32[2048]{0:T(1024)S(1)}, f32[2048]{0:T(1024)}, u32[]{:S(2)}) copy-start(f32[2048]{0:T(1024)} %fusion.42) | copy-start | bytes 24580
  107.2 41.5 %copy-start.30 = (f32[48]{0:T(128)S(1)}, f32[48]{0:T(128)}, u32[]{:S(2)}) copy-start(f32[48]{0:T(128)} %copy-done.29) | copy-start | bytes 580
  107.9 11.2 %collective-permute-start = (bf16[1024,48]{0,1:T(8,128)(2,1)S(1)}, bf16[1024,48]{0,1:T(8,128)(2,1)S(1)}, u32[]{:S(2)}, u32[]{:S(2)}) collective-permute-start(bf16[1024,48]{0,1:T(8,128)(2,1)S(1)} %fusion.75), channel_id=1, source_target_pairs={{0,128},{128,0},{1,129},{129,1},{2,130},{130,2},{3,131},{131,3},{4... | collective-permute-start | bytes 294920 | tf_op jit(solution)/shard_map/ppermute | solution.py:12
  118.8 37.1 %copy-start.15 = (s32[2048]{0:T(1024)}, s32[2048]{0:T(1024)S(1)}, u32[]{:S(2)}) copy-start(s32[2048]{0:T(1024)S(1)} %get-tuple-element.11) | copy-start | bytes 24580
  119.1 29.5 %copy-start.5 = (bf16[1024,48]{0,1:T(8,128)(2,1)}, bf16[1024,48]{0,1:T(8,128)(2,1)S(1)}, u32[]{:S(2)}) copy-start(bf16[1024,48]{0,1:T(8,128)(2,1)S(1)} %collective-permute-done) | copy-start | bytes 294916
  182.0 5.3 %copy-start.9 = (s32[1,1,1024,2]{2,3,1,0:T(2,128)S(1)}, s32[1,1,1024,2]{2,3,1,0:T(2,128)}, u32[]{:S(2)}) copy-start(s32[1,1,1024,2]{2,3,1,0:T(2,128)} %get-tuple-element.37) | copy-start | bytes 24580
  183.5 14.2 %all-to-all-start.3 = ((bf16[16,2,12288]{2,1,0:T(2,128)(2,1)}), bf16[16,2,12288]{2,1,0:T(2,128)(2,1)S(1)}, u32[]{:S(2)}, u32[]{:S(2)}) async-start(bf16[16,2,12288]{2,1,0:T(2,128)(2,1)} %reshape.211), calls=%async_computation.3 | async-start | bytes 1572864 | tf_op jit(solution)/shard_map/all_to_all | solution.py:64
  187.8 2.0 copy-start.16
  202.8 2.5 copy-start.20
  205.3 7.6 %copy-start.35 = (pred[2048]{0:T(1024)(128)(4,1)S(1)}, pred[2048]{0:T(1024)(128)(4,1)}, u32[]{:S(2)}) copy-start(pred[2048]{0:T(1024)(128)(4,1)} %get-tuple-element.10) | copy-start | bytes 6148
  214.5 1.5 copy-start.6
  214.5 1.5 copy-start.21
  214.5 1.5 copy-start.22
  214.5 11.4 %copy-start.39 = (f32[2048]{0:T(1024)S(1)}, f32[2048]{0:T(1024)}, u32[]{:S(2)}) copy-start(f32[2048]{0:T(1024)} %fusion.41) | copy-start | bytes 24580
  215.3 41.1 %copy-start.31 = (f32[48]{0:T(128)S(1)}, f32[48]{0:T(128)}, u32[]{:S(2)}) copy-start(f32[48]{0:T(128)} %copy-done.29) | copy-start | bytes 580
  216.0 10.9 %collective-permute-start.1 = (bf16[1024,48]{0,1:T(8,128)(2,1)S(1)}, bf16[1024,48]{0,1:T(8,128)(2,1)S(1)}, u32[]{:S(2)}, u32[]{:S(2)}) collective-permute-start(bf16[1024,48]{0,1:T(8,128)(2,1)S(1)} %fusion.60), channel_id=1, source_target_pairs={{0,128},{128,0},{1,129},{129,1},{2,130},{130,2},{3,131},{131,3},{4... | collective-permute-start | bytes 294920 | tf_op jit(solution)/shard_map/ppermute | solution.py:12
  226.5 37.1 %copy-start.13 = (s32[2048]{0:T(1024)}, s32[2048]{0:T(1024)S(1)}, u32[]{:S(2)}) copy-start(s32[2048]{0:T(1024)S(1)} %get-tuple-element.9) | copy-start | bytes 24580
  226.9 29.5 %copy-start.3 = (bf16[1024,48]{0,1:T(8,128)(2,1)}, bf16[1024,48]{0,1:T(8,128)(2,1)S(1)}, u32[]{:S(2)}) copy-start(bf16[1024,48]{0,1:T(8,128)(2,1)S(1)} %collective-permute-done.1) | copy-start | bytes 294916
  291.0 14.4 %all-to-all-start.5 = ((bf16[16,2,12288]{2,1,0:T(2,128)(2,1)}), bf16[16,2,12288]{2,1,0:T(2,128)(2,1)S(1)}, u32[]{:S(2)}, u32[]{:S(2)}) async-start(bf16[16,2,12288]{2,1,0:T(2,128)(2,1)} %reshape.213), calls=%async_computation.5 | async-start | bytes 1572864 | tf_op jit(solution)/shard_map/all_to_all | solution.py:64
  295.5 2.1 copy-start.14
  295.5 2.1 copy-start.17
  295.5 2.0 copy-start.18
  313.0 7.6 %copy-start.34 = (pred[2048]{0:T(1024)(128)(4,1)S(1)}, pred[2048]{0:T(1024)(128)(4,1)}, u32[]{:S(2)}) copy-start(pred[2048]{0:T(1024)(128)(4,1)} %get-tuple-element.8) | copy-start | bytes 6148
  322.2 1.5 copy-start.4
  322.2 1.5 copy-start.25
  322.2 1.5 copy-start.26
  322.2 11.4 %copy-start.38 = (f32[2048]{0:T(1024)S(1)}, f32[2048]{0:T(1024)}, u32[]{:S(2)}) copy-start(f32[2048]{0:T(1024)} %fusion.40) | copy-start | bytes 24580
  323.0 41.1 %copy-start.32 = (f32[48]{0:T(128)S(1)}, f32[48]{0:T(128)}, u32[]{:S(2)}) copy-start(f32[48]{0:T(128)} %copy-done.29) | copy-start | bytes 580
  323.7 10.9 %collective-permute-start.2 = (bf16[1024,48]{0,1:T(8,128)(2,1)S(1)}, bf16[1024,48]{0,1:T(8,128)(2,1)S(1)}, u32[]{:S(2)}, u32[]{:S(2)}) collective-permute-start(bf16[1024,48]{0,1:T(8,128)(2,1)S(1)} %fusion.65), channel_id=1, source_target_pairs={{0,128},{128,0},{1,129},{129,1},{2,130},{130,2},{3,131},{131,3},{4... | collective-permute-start | bytes 294920 | tf_op jit(solution)/shard_map/ppermute | solution.py:12
  334.6 29.5 %copy-start.7 = (bf16[1024,48]{0,1:T(8,128)(2,1)}, bf16[1024,48]{0,1:T(8,128)(2,1)S(1)}, u32[]{:S(2)}) copy-start(bf16[1024,48]{0,1:T(8,128)(2,1)S(1)} %collective-permute-done.2) | copy-start | bytes 294916
  398.7 14.0 %all-to-all-start.7 = ((bf16[16,2,12288]{2,1,0:T(2,128)(2,1)}), bf16[16,2,12288]{2,1,0:T(2,128)(2,1)S(1)}, u32[]{:S(2)}, u32[]{:S(2)}) async-start(bf16[16,2,12288]{2,1,0:T(2,128)(2,1)} %reshape.215), calls=%async_computation.7 | async-start | bytes 1572864 | tf_op jit(solution)/shard_map/all_to_all | solution.py:64
  420.3 7.6 %copy-start.36 = (pred[2048]{0:T(1024)(128)(4,1)S(1)}, pred[2048]{0:T(1024)(128)(4,1)}, u32[]{:S(2)}) copy-start(pred[2048]{0:T(1024)(128)(4,1)} %get-tuple-element.6) | copy-start | bytes 6148
  429.5 1.4 copy-start.8
  429.5 1.4 copy-start.23
  429.5 1.4 copy-start.24
  431.0 10.9 %collective-permute-start.3 = (bf16[1024,48]{0,1:T(8,128)(2,1)S(1)}, bf16[1024,48]{0,1:T(8,128)(2,1)S(1)}, u32[]{:S(2)}, u32[]{:S(2)}) collective-permute-start(bf16[1024,48]{0,1:T(8,128)(2,1)S(1)} %fusion.70), channel_id=1, source_target_pairs={{0,128},{128,0},{1,129},{129,1},{2,130},{130,2},{3,131},{131,3},{4... | collective-permute-start | bytes 294920 | tf_op jit(solution)/shard_map/ppermute | solution.py:12
where the time goes:
time: 450 us; the launch traced here: 443 us
  blocking collectives  163 us (36%)
  local copies, waits for them, and re-layouts  75.2 us (17%)
  starting transfers between devices  59.1 us (13%)
  matrix products  57.2 us (13%)
  other arithmetic  44.2 us (10%)
  waiting for transfers between devices  43.2 us (10%)
    psum x4, blocking collectives, per_device(): sum_squares = lax.psum(jnp.sum(widened * widened, axis=1), 'expert')  123 us
    ppermute x4, starting transfers between devices, passed_along(): lax.ppermute(array, axis, [(i, (i + by) % devices) for i in range(devices)])  40.1 us
    all_to_all x3, blocking collectives, per_device(): lax.all_to_all(packed, 'expert', split_axis=0, concat_axis=2, tiled=True)[0]  39.8 us
    all_to_all x4, waiting for transfers between devices, per_device(): lax.all_to_all(outcome[None], 'expert', split_axis=2, concat_axis=0, tile...  31.3 us
    gather x4, local copies, waits for them, and re-layouts, per_device(): jnp.take(combined, slot_key, axis=0).reshape(row_count, 2, width_local)  30.3 us
    unnamed x108, local copies, waits for them, and re-layouts  27.9 us
    dot_general x4, matrix products, per_device(): jnp.dot(selector, doubled, preferred_element_type=jnp.float32)  26.7 us
    unnamed x4, other arithmetic  21.8 us
  transfers between devices with their start and end apart: 9, of which 9 were waited for; matrix products, arithmetic and copies ran while one was open for 3% of the time, Pallas kernels for 0%

commit v1 on v0

v1 whole, which is shorter than its diff:
```python
import functools

import jax
import jax.numpy as jnp
from jax import lax
from jax.experimental import pallas as pl
from jax.experimental.pallas import tpu as pltpu
from jax.sharding import PartitionSpec as P

D = 768
STOPS = 4
GROUPS = 4
SIDE = 4
SLICE = 48
MESH = pl.DeviceIdType.MESH


def kernel(
    lanes,
    tokens_ref, gain_ref, weight_ref, gate_ref, up_ref, down_ref,
    out_ref,
    gathered, partial, returned, summed, last, held, final, gain_all,
    gate_t, up_t, down_t, raw,
    recv_sem, send_sem, final_recv, final_send, gain_recv, gain_send, load_sem,
):
    section = lax.axis_index("section")
    chip = lax.axis_index("expert")
    plane = lax.axis_index("dp")
    y, x = chip // SIDE, lax.rem(chip, SIDE)

    def device(core, row, column):
        return (core, row * SIDE + column, plane)

    other = 1 - section
    y_peers = [lax.rem(y + step, SIDE) for step in range(1, SIDE)]
    x_peers = [lax.rem(x + step, SIDE) for step in range(1, SIDE)]

    loads = [
        pltpu.make_async_copy(source, raw.at[i], load_sem.at[i])
        for i, source in enumerate((gate_ref, up_ref, down_ref))
    ]
    for load in loads:
        load.start()

    barrier = pltpu.get_barrier_semaphore()
    partners = [device(other, y, x)]
    for core in (section, other):
        partners += [device(core, row, x) for row in y_peers]
        partners += [device(core, y, column) for column in x_peers]
    for partner in partners:
        pl.semaphore_signal(barrier, inc=1, device_id=partner, device_id_type=MESH)
    pl.semaphore_wait(barrier, len(partners))

    def send(source, target, send_at, recv_at, to):
        pltpu.make_async_remote_copy(
            src_ref=source, dst_ref=target, send_sem=send_at, recv_sem=recv_at,
            device_id=to, device_id_type=MESH,
        ).start()

    def wait_blocks(sem, rows, blocks):
        room = gathered.at[0, 0, 0] if rows == 16 else None
        del room
        view = returned.at[0, 0].reshape(2 * SIDE * SIDE, SLICE, lanes).at[pl.ds(0, blocks)]
        pltpu.make_async_copy(view, view, sem).wait()

    for group in range(GROUPS):
        to_recv, to_send = recv_sem.at[0, 0, group], send_sem.at[0, 0, group]
        for half in range(2):
            block = tokens_ref.at[group, half]
            mine = gathered.at[0, group, half, y, x]
            pltpu.make_async_copy(block, mine, to_recv).start()
            for peer in y_peers if half == 0 else x_peers:
                to = device(section, peer, x) if half == 0 else device(section, y, peer)
                send(block, mine, to_send, to_recv, to)
    pltpu.make_async_copy(gain_ref, gain_all.at[y, x], gain_recv.at[0]).start()
    for peer in y_peers:
        send(gain_ref, gain_all.at[y, x], gain_send.at[0], gain_recv.at[0], device(section, peer, x))

    for i, target in enumerate((gate_t, up_t, down_t)):
        loads[i].wait()
        target[...] = raw[i].T

    def wait_gain(sem, blocks):
        view = gain_all.reshape(SIDE * SIDE, SLICE, 128).at[pl.ds(0, blocks)]
        pltpu.make_async_copy(view, view, sem).wait()

    wait_gain(gain_recv.at[0], 4)
    for peer in x_peers:
        send(gain_all.at[:, x], gain_all.at[:, x], gain_send.at[1], gain_recv.at[1], device(section, y, peer))

    def spread(t, g):
        wait_blocks(recv_sem.at[0, t, g], 0, 8)
        to_recv, to_send = recv_sem.at[1, t, g], send_sem.at[1, t, g]
        for i in range(3):
            column = gathered.at[t, g, 0, :, x]
            send(column, column, to_send, to_recv, device(section, y, x_peers[i]))
            row = gathered.at[t, g, 1, y]
            send(row, row, to_send, to_recv, device(section, y_peers[i], x))

    def compute(t, g):
        wait_blocks(recv_sem.at[1, t, g], 0, 24)

        @pl.when((t == 0) & (g == 0))
        def _():
            wait_gain(gain_recv.at[1], 12)

        acts = jnp.concatenate(
            [gathered[t, g, half].reshape(D, lanes) for half in range(2)], axis=1
        ).astype(jnp.float32)
        inverse = lax.rsqrt(jnp.sum(acts * acts, axis=0, keepdims=True) / D + 1e-05)
        gain = gain_all[...].reshape(D, 128).astype(jnp.float32)
        gain = jnp.concatenate([gain] * (2 * lanes // 128), axis=1)
        normed = (acts * inverse * gain).astype(jnp.bfloat16)
        gate_val = jnp.dot(gate_t[...], normed, preferred_element_type=jnp.float32)
        up_val = jnp.dot(up_t[...], normed, preferred_element_type=jnp.float32)
        hidden = (jax.nn.silu(gate_val) * up_val).astype(jnp.bfloat16)
        outcome = jnp.dot(down_t[...], hidden, preferred_element_type=jnp.float32)
        outcome = (outcome * weight_ref[t, g]).astype(jnp.bfloat16)
        for half in range(2):
            partial[t, g, half] = outcome[:, half * lanes:(half + 1) * lanes].reshape(SIDE, SIDE, SLICE, lanes)
        to_recv, to_send = recv_sem.at[2, t, g], send_sem.at[2, t, g]
        for i in range(3):
            send(partial.at[t, g, 0, :, x_peers[i]], returned.at[t, g, 0, x], to_send, to_recv,
                 device(section, y, x_peers[i]))
            send(partial.at[t, g, 1, y_peers[i]], returned.at[t, g, 1, y], to_send, to_recv,
                 device(section, y_peers[i], x))

    def collect(t, g):
        wait_blocks(recv_sem.at[2, t, g], 0, 24)
        total = partial[t, g, 0, :, x].astype(jnp.float32)
        for peer in x_peers:
            total = total + returned[t, g, 0, peer].astype(jnp.float32)
        summed[t, g, 0] = total.astype(jnp.bfloat16)
        total = partial[t, g, 1, y].astype(jnp.float32)
        for peer in y_peers:
            total = total + returned[t, g, 1, peer].astype(jnp.float32)
        summed[t, g, 1] = total.astype(jnp.bfloat16)
        to_recv, to_send = recv_sem.at[3, t, g], send_sem.at[3, t, g]
        for i in range(3):
            send(summed.at[t, g, 0, y_peers[i]], last.at[t, g, 0, y], to_send, to_recv,
                 device(section, y_peers[i], x))
            send(summed.at[t, g, 1, x_peers[i]], last.at[t, g, 1, x], to_send, to_recv,
                 device(section, y, x_peers[i]))

    def finish(t, g):
        wait_blocks(recv_sem.at[3, t, g], 0, 6)
        for half in range(2):
            own, peers = (y, y_peers) if half == 0 else (x, x_peers)
            total = summed[t, g, half, own].astype(jnp.float32)
            for peer in peers:
                total = total + last[t, g, half, peer].astype(jnp.float32)
            total = gathered[t, g, half, y, x].astype(jnp.float32) + total
            held[t, g, half] = total.astype(jnp.bfloat16)

        @pl.when(t < STOPS - 1)
        def _():
            later = jnp.minimum(t + 1, STOPS - 1)
            to_recv, to_send = recv_sem.at[0, later, g], send_sem.at[0, later, g]
            for half in range(2):
                target = gathered.at[later, g, half, y, x]
                send(held.at[t, g, half], target, to_send, to_recv, device(other, y, x))
                for peer in y_peers if half == 0 else x_peers:
                    to = device(other, peer, x) if half == 0 else device(other, y, peer)
                    send(held.at[t, g, half], target, to_send, to_recv, to)

        @pl.when(t == STOPS - 1)
        def _():
            send(held.at[t, g], final.at[g], final_send.at[g], final_recv.at[g], device(other, y, x))

    stages = (spread, compute, collect, finish)
    count = len(stages)

    def tick(now, carry):
        for k, stage in enumerate(stages):
            g = lax.rem(now - k + count, count)
            n = now - g

            @pl.when((n >= 0) & (n < count * STOPS))
            def _(stage=stage, g=g, n=n):
                stage(jnp.maximum(n, 0) // count, g)
        return carry

    lax.fori_loop(0, count * STOPS + GROUPS - 1, tick, 0)

    for g in range(GROUPS):
        wait_blocks(final_recv.at[g], 0, 2)
        wait_blocks(final_send.at[g], 0, 2)
        out_ref[g] = final[g]
    wait_gain(gain_send.at[0], 3)
    wait_gain(gain_send.at[1], 12)

    def settle(t, carry):
        for g in range(GROUPS):
            for k, blocks in enumerate((8, 24, 24, 6)):
                if k:
                    wait_blocks(send_sem.at[k, t, g], 0, blocks)

            @pl.when(t == 0)
            def _():
                wait_blocks(send_sem.at[0, 0, g], 0, 6)

            @pl.when(t > 0)
            def _():
                wait_blocks(send_sem.at[0, t, g], 0, 8)
        return carry

    lax.fori_loop(0, STOPS, settle, 0)


def per_device(tokens, norm_gain, w_gate, w_up, w_down, expert_ids, gate_logits):
    rows, width = tokens.shape[1:]
    lanes = rows // (2 * GROUPS)
    split = tokens[0].reshape(GROUPS, 2, lanes, width).transpose(0, 1, 3, 2)
    gain = jnp.broadcast_to(norm_gain[0][:, None], (width, 128))
    expert = lax.axis_index("expert") // 2
    ids, logits = expert_ids[0], gate_logits[0]
    weight_one = jax.nn.sigmoid(logits[..., 0] - logits[..., 1])
    weight_two = jax.nn.sigmoid(logits[..., 1] - logits[..., 0])
    weight = jnp.where(ids[..., 0] == expert, weight_one, 0.0) + jnp.where(ids[..., 1] == expert, weight_two, 0.0)
    weight = weight.reshape(STOPS, GROUPS, 1, 2 * lanes)
    block = (STOPS, GROUPS, 2)
    vmem = pl.BlockSpec(memory_space=pltpu.VMEM)
    out = pl.pallas_call(
        functools.partial(kernel, lanes),
        out_shape=jax.ShapeDtypeStruct((GROUPS, 2, width, lanes), jnp.bfloat16),
        in_specs=[vmem] * 3 + [pl.BlockSpec(memory_space=pl.ANY)] * 3,
        out_specs=vmem,
        scratch_shapes=[
            pltpu.VMEM(block + (SIDE, SIDE, width, lanes), jnp.bfloat16),
            pltpu.VMEM(block + (SIDE, SIDE, width, lanes), jnp.bfloat16),
            pltpu.VMEM(block + (SIDE, SIDE, width, lanes), jnp.bfloat16),
            pltpu.VMEM(block + (SIDE, width, lanes), jnp.bfloat16),
            pltpu.VMEM(block + (SIDE, width, lanes), jnp.bfloat16),
            pltpu.VMEM(block + (width, lanes), jnp.bfloat16),
            pltpu.VMEM((GROUPS, 2, width, lanes), jnp.bfloat16),
            pltpu.VMEM((SIDE, SIDE, width, 128), jnp.bfloat16),
            pltpu.VMEM((D, D), jnp.bfloat16),
            pltpu.VMEM((D, D), jnp.bfloat16),
            pltpu.VMEM((D, D), jnp.bfloat16),
            pltpu.VMEM((3, D, D), jnp.bfloat16),
            pltpu.SemaphoreType.DMA((4, STOPS, GROUPS)),
            pltpu.SemaphoreType.DMA((4, STOPS, GROUPS)),
            pltpu.SemaphoreType.DMA((GROUPS,)),
            pltpu.SemaphoreType.DMA((GROUPS,)),
            pltpu.SemaphoreType.DMA((2,)),
            pltpu.SemaphoreType.DMA((2,)),
            pltpu.SemaphoreType.DMA((3,)),
        ],
        compiler_params=pltpu.CompilerParams(
            collective_id=0, has_side_effects=True, vmem_limit_bytes=56 << 20
        ),
    )(split, gain, weight, w_gate[0], w_up[0], w_down[0])
    return out.transpose(0, 1, 3, 2).reshape(1, rows, width)


def solution(mesh):
    placed = (
        P("section", "dp", "expert"),
        P("section", "expert"),
        P("section", None, "expert"),
        P("section", None, "expert"),
        P("section", "expert", None),
        P("section", None, "dp", None),
        P("section", None, "dp", None),
    )
    return jax.shard_map(
        per_device,
        mesh=mesh,
        in_specs=placed,
        out_specs=P("section", "dp", "expert"),
        check_vma=False,
    )
```

time: 450 us -> 144 us (0.32); the launches traced: 443 us -> 143 us
  blocking collectives: 163 us -> 0 us
  Pallas kernels: 0 us -> 137 us
  local copies, waits for them, and re-layouts: 75.2 us -> 4.58 us
  starting transfers between devices: 59.1 us -> 0 us
  matrix products: 57.2 us -> 0 us
  waiting for transfers between devices: 43.2 us -> 0 us
  other arithmetic: 44.2 us -> 1.53 us
    pallas_call x0 -> x1, Pallas kernels: none -> 137 us  [per_device(): pl.pallas_call(functools.partial(kernel, lanes), out_shape=jax.ShapeDtype...]
    psum x4 -> x0, blocking collectives: 123 us -> none  [per_device(): sum_squares = lax.psum(jnp.sum(widened * widened, axis=1), 'expert')]
    dot_general x16 -> x0, matrix products: 57.2 us -> none  [the longest x4 26.7 us: per_device(): jnp.dot(selector, doubled, preferred_element_type=jnp.float32)]
    all_to_all x5 -> x0, waiting for transfers between devices: 41.2 us -> none  [the longest x4 31.3 us: per_device(): lax.all_to_all(outcome[None], 'expert', split_axis=2, concat_axis=0, tile...]
    ppermute x4 -> x0, starting transfers between devices: 40.1 us -> none  [passed_along(): lax.ppermute(array, axis, [(i, (i + by) % devices) for i in range(devices)])]
    all_to_all x3 -> x0, blocking collectives: 39.8 us -> none  [per_device(): lax.all_to_all(packed, 'expert', split_axis=0, concat_axis=2, tiled=True)[0]]
    gather x4 -> x0, local copies, waits for them, and re-layouts: 30.3 us -> none  [per_device(): jnp.take(combined, slot_key, axis=0).reshape(row_count, 2, width_local)]
    unnamed x108 -> x0, local copies, waits for them, and re-layouts: 27.9 us -> none
  transfers between devices with their start and end apart: 9 -> 0, of which waited for: 9 -> 0; matrix products, arithmetic and copies ran while one was open for 3% -> 0% of each run, Pallas kernels for 0% -> 0%
where the time goes in v1:
time: 144 us; the launch traced here: 143 us
  Pallas kernels  137 us (95%)
  local copies, waits for them, and re-layouts  4.58 us (3%)
  other arithmetic  1.53 us (1%)
    pallas_call x1, Pallas kernels, per_device(): pl.pallas_call(functools.partial(kernel, lanes), out_shape=jax.ShapeDtype...  137 us

profile of v1, /device:TPU:1, one launch (start us, length us, event | category | flops | bytes accessed | tf_op | source)
XLA Modules:
  0.0 143.4 jit_solution(1023347136274180702)
XLA Ops:
  0.0 1.3 broadcast_in_dim.13.gain_ref
  1.3 1.5 %fusion = f32[4,1024,1]{1,2,0:T(1,128)} fusion(s32[4,1024,2]{1,2,0:T(2,128)} %bitcast.21, f32[4,1024,2]{1,2,0:T(2,128)} %bitcast.22, s32[]{:T(128)S(6)} %select_n.26), kind=kLoop, calls=%fused_computation.3 | loop fusion | flops 53248 | bytes 81924 | tf_op jit(solution)/shard_map/add | solution.py:219
  2.9 0.9 reshape_squeeze.3
  3.8 0.7 copy.11
  4.5 137.3 %shard_map.73 = bf16[4,2,48,128]{3,2,1,0:T(8,128)(2,1)} custom-call(bf16[4,2,48,128]{3,2,1,0:T(8,128)(2,1)} %bitcast.18, bf16[48,128]{1,0:T(8,128)(2,1)} %broadcast_in_dim.13.gain_ref, f32[4,4,1,256]{3,2,1,0:T(1,128)} %bitcast.20, bf16[768,768]{1,0:T(8,128)(2,1)} %bitcast.15, bf16[768,768]{1,0:T(8,128)(2,1)} %bitcast.16, bf16[768,768]{1,0:T(8,128)(2,1)} %bitcast.17), custom_call_target="tpu_custom_call" | custom-call | tf_op jit(solution)/shard_map/pallas_call | solution.py:223
  141.7 1.0 copy.9
  142.7 0.7 reshape.104

commit v2 on v1

v2 whole, which is shorter than its diff:
```python
import jax
import jax.numpy as jnp
from jax import lax
from jax.experimental import pallas as pl
from jax.experimental.pallas import tpu as pltpu
from jax.sharding import PartitionSpec as P

D = 768
STOPS = 4
GROUPS = 4
SIDE = 4
SLICE = 48
PIECE = 256
MESH = pl.DeviceIdType.MESH


def kernel(
    tokens_ref, gain_ref, ids_ref, logits_ref, gate_ref, up_ref, down_ref,
    out_ref,
    gathered, partial, returned, summed, last, held, final, gain_own, gain_all, weight,
    gate_t, up_t, down_t, raw,
    recv_sem, send_sem, final_recv, final_send, gain_recv, gain_send, load_sem,
):
    section = lax.axis_index("section")
    chip = lax.axis_index("expert")
    plane = lax.axis_index("dp")
    y, x = chip // SIDE, lax.rem(chip, SIDE)
    lanes = gathered.shape[-1]

    def device(core, row, column):
        return (core, row * SIDE + column, plane)

    other = 1 - section
    y_peers = [lax.rem(y + step, SIDE) for step in range(1, SIDE)]
    x_peers = [lax.rem(x + step, SIDE) for step in range(1, SIDE)]

    barrier = pltpu.get_barrier_semaphore()
    partners = [device(other, y, x)]
    for core in (section, other):
        partners += [device(core, row, x) for row in y_peers]
        partners += [device(core, y, column) for column in x_peers]
    for partner in partners:
        pl.semaphore_signal(barrier, inc=1, device_id=partner, device_id_type=MESH)
    loads = [
        pltpu.make_async_copy(source, raw.at[i], load_sem.at[i])
        for i, source in enumerate((gate_ref, up_ref, down_ref))
    ]
    for load in loads:
        load.start()
    gain_row = jnp.broadcast_to(gain_ref[...].astype(jnp.float32), (128, SLICE))
    gain_own[...] = gain_row.T.astype(jnp.bfloat16)
    pl.semaphore_wait(barrier, len(partners))

    def send(source, target, send_at, recv_at, to):
        pltpu.make_async_remote_copy(
            src_ref=source, dst_ref=target, send_sem=send_at, recv_sem=recv_at,
            device_id=to, device_id_type=MESH,
        ).start()

    def wait_blocks(sem, blocks):
        view = gathered.at[0, 0].reshape(2 * SIDE * SIDE, SLICE, lanes).at[pl.ds(0, blocks)]
        pltpu.make_async_copy(view, view, sem).wait()

    def wait_gain(sem, blocks):
        view = gain_all.reshape(SIDE * SIDE, SLICE, 128).at[pl.ds(0, blocks)]
        pltpu.make_async_copy(view, view, sem).wait()

    def chip_at(half, on_line, across):
        return (across, on_line) if half == 0 else (on_line, across)

    mine = [(x, y), (y, x)]
    line_peers = [x_peers, y_peers]
    before = [lax.rem(place[1] + SIDE - 1, SIDE) for place in mine]
    after = [lax.rem(place[1] + 1, SIDE) for place in mine]
    opposite = [lax.rem(place[1] + 2, SIDE) for place in mine]

    def line(ref, half, across):
        return ref.at[across] if half == 0 else ref.at[:, across]

    def spot(ref, half, on_line, across):
        row, column = chip_at(half, on_line, across)
        return ref.at[row, column]

    def to_chip(core, half, on_line, across):
        return device(core, *chip_at(half, on_line, across))

    def first_step(source, t, g, half, core):
        target = gathered.at[t, g, half, y, x]
        to_recv, to_send = recv_sem.at[0, t, g], send_sem.at[0, t, g]
        on_line, across = mine[half]
        for peer in line_peers[half]:
            send(source, target, to_send, to_recv, to_chip(core, half, peer, across))
        send(source, target, to_send, to_recv, to_chip(core, half, on_line, opposite[half]))

    for group in range(GROUPS):
        for half in range(2):
            block = tokens_ref.at[:, pl.ds((2 * group + half) * lanes, lanes)]
            pltpu.make_async_copy(block, gathered.at[0, group, half, y, x], recv_sem.at[0, 0, group]).start()
            first_step(block, 0, group, half, section)
        if group == 0:
            pltpu.make_async_copy(gain_own, gain_all.at[y, x], gain_recv.at[0]).start()
            for peer in y_peers:
                send(gain_own, gain_all.at[y, x], gain_send.at[0], gain_recv.at[0], device(section, peer, x))

    expert = chip // 2
    for t in range(STOPS):
        for g in range(GROUPS):
            span = pl.ds(2 * g * lanes, 2 * lanes)
            ids, logits = ids_ref[t, :, span], logits_ref[t, :, span]
            one = jax.nn.sigmoid(logits[0:1] - logits[1:2])
            two = jax.nn.sigmoid(logits[1:2] - logits[0:1])
            weight[t, g] = jnp.where(ids[0:1] == expert, one, 0.0) + jnp.where(ids[1:2] == expert, two, 0.0)

    def spread(t, g):
        wait_blocks(recv_sem.at[0, t, g], 10)
        to_recv, to_send = recv_sem.at[1, t, g], send_sem.at[1, t, g]
        for half in range(2):
            on_line, across = mine[half]
            own_line = line(gathered.at[t, g, half], half, across)
            for beside in (before[half], after[half]):
                send(own_line, own_line, to_send, to_recv, to_chip(section, half, on_line, beside))
        for half in range(2):
            on_line, across = mine[half]
            far = spot(gathered.at[t, g, half], half, on_line, opposite[half])
            for peer in line_peers[half]:
                send(far, far, to_send, to_recv, to_chip(section, half, peer, across))

    def compute(t, g):
        wait_blocks(recv_sem.at[1, t, g], 22)
        acts = jnp.concatenate(
            [gathered[t, g, half].reshape(D, lanes) for half in range(2)], axis=1
        ).astype(jnp.float32)
        inverse = lax.rsqrt(jnp.sum(acts * acts, axis=0, keepdims=True) / D + 1e-05)
        gain = gain_all[...].reshape(D, 128).astype(jnp.float32)
        gain = jnp.concatenate([gain] * (2 * lanes // 128), axis=1)
        normed = (acts * inverse * gain).astype(jnp.bfloat16)
        pieces = []
        for start in range(0, D, PIECE):
            gate_val = jnp.dot(gate_t[start:start + PIECE], normed, preferred_element_type=jnp.float32)
            up_val = jnp.dot(up_t[start:start + PIECE], normed, preferred_element_type=jnp.float32)
            pieces.append((jax.nn.silu(gate_val) * up_val).astype(jnp.bfloat16))
        hidden = jnp.concatenate(pieces, axis=0)
        outcome = jnp.dot(down_t[...], hidden, preferred_element_type=jnp.float32)
        outcome = (outcome * weight[t, g]).astype(jnp.bfloat16)
        for half in range(2):
            partial[t, g, half] = outcome[:, half * lanes:(half + 1) * lanes].reshape(SIDE, SIDE, SLICE, lanes)
        to_recv, to_send = recv_sem.at[2, t, g], send_sem.at[2, t, g]
        for half in range(2):
            on_line, across = mine[half]
            for beside, slot in ((before[half], 1), (after[half], 0)):
                send(line(partial.at[t, g, half], half, beside), returned.at[t, g, half, slot], to_send, to_recv,
                     to_chip(section, half, on_line, beside))
        for half in range(2):
            on_line, across = mine[half]
            for peer in line_peers[half]:
                send(spot(partial.at[t, g, half], half, peer, opposite[half]), returned.at[t, g, half, 2, on_line],
                     to_send, to_recv, to_chip(section, half, peer, across))

    def collect(t, g):
        wait_blocks(recv_sem.at[2, t, g], 22)
        to_recv, to_send = recv_sem.at[3, t, g], send_sem.at[3, t, g]
        for half in range(2):
            on_line, across = mine[half]
            total = line(partial.at[t, g, half], half, across)[...].astype(jnp.float32)
            total = total + returned[t, g, half, 0].astype(jnp.float32) + returned[t, g, half, 1].astype(jnp.float32)
            summed[t, g, half, 0:SIDE] = total.astype(jnp.bfloat16)
            total = spot(partial.at[t, g, half], half, on_line, opposite[half])[...].astype(jnp.float32)
            for peer in line_peers[half]:
                total = total + returned[t, g, half, 2, peer].astype(jnp.float32)
            summed[t, g, half, SIDE] = total.astype(jnp.bfloat16)
            for peer in line_peers[half]:
                send(summed.at[t, g, half, peer], last.at[t, g, half, on_line], to_send, to_recv,
                     to_chip(section, half, peer, across))
            send(summed.at[t, g, half, SIDE], last.at[t, g, half, SIDE], to_send, to_recv,
                 to_chip(section, half, on_line, opposite[half]))

    def finish(t, g):
        wait_blocks(recv_sem.at[3, t, g], 8)
        for half in range(2):
            on_line, across = mine[half]
            total = summed[t, g, half, on_line].astype(jnp.float32) + last[t, g, half, SIDE].astype(jnp.float32)
            for peer in line_peers[half]:
                total = total + last[t, g, half, peer].astype(jnp.float32)
            total = gathered[t, g, half, y, x].astype(jnp.float32) + total
            held[t, g, half] = total.astype(jnp.bfloat16)

        @pl.when(t < STOPS - 1)
        def _():
            later = jnp.minimum(t + 1, STOPS - 1)
            for half in range(2):
                block = held.at[t, g, half]
                first_step(block, later, g, half, other)
                send(block, gathered.at[later, g, half, y, x], send_sem.at[0, later, g], recv_sem.at[0, later, g],
                     device(other, y, x))

        @pl.when(t == STOPS - 1)
        def _():
            send(held.at[t, g], final.at[g], final_send.at[g], final_recv.at[g], device(other, y, x))

    def each_group(stage, t):
        def one(g, carry):
            stage(t, g)
            return carry
        lax.fori_loop(0, GROUPS, one, 0)

    each_group(spread, 0)
    wait_gain(gain_recv.at[0], 4)
    for peer in x_peers:
        send(gain_all.at[:, x], gain_all.at[:, x], gain_send.at[1], gain_recv.at[1], device(section, y, peer))
    for i, target in enumerate((gate_t, up_t, down_t)):
        loads[i].wait()
        target[...] = raw[i].T
    wait_gain(gain_recv.at[1], 12)

    def stop(t, carry):
        each_group(compute, t)
        each_group(collect, t)
        each_group(finish, t)

        @pl.when(t < STOPS - 1)
        def _():
            each_group(spread, jnp.minimum(t + 1, STOPS - 1))
        return carry

    lax.fori_loop(0, STOPS, stop, 0)

    def settle(t, carry):
        for g in range(GROUPS):
            for k, blocks in ((1, 22), (2, 22), (3, 8)):
                wait_blocks(send_sem.at[k, t, g], blocks)

            @pl.when(t == 0)
            def _():
                wait_blocks(send_sem.at[0, 0, g], 8)

            @pl.when(t > 0)
            def _():
                wait_blocks(send_sem.at[0, t, g], 10)
        return carry

    lax.fori_loop(0, STOPS, settle, 0)
    wait_gain(gain_send.at[0], 3)
    wait_gain(gain_send.at[1], 12)
    for g in range(GROUPS):
        wait_blocks(final_send.at[g], 2)
        wait_blocks(final_recv.at[g], 2)
        for half in range(2):
            out_ref[:, (2 * g + half) * lanes:(2 * g + half + 1) * lanes] = final[g, half]


def per_device(tokens, norm_gain, w_gate, w_up, w_down, expert_ids, gate_logits):
    rows, width = tokens.shape[1:]
    lanes = rows // (2 * GROUPS)
    block = (STOPS, GROUPS, 2)
    vmem = pl.BlockSpec(memory_space=pltpu.VMEM)
    out = pl.pallas_call(
        kernel,
        out_shape=jax.ShapeDtypeStruct((width, rows), jnp.bfloat16),
        in_specs=[vmem] * 4 + [pl.BlockSpec(memory_space=pl.ANY)] * 3,
        out_specs=vmem,
        scratch_shapes=[
            pltpu.VMEM(block + (SIDE, SIDE, width, lanes), jnp.bfloat16),
            pltpu.VMEM(block + (SIDE, SIDE, width, lanes), jnp.bfloat16),
            pltpu.VMEM(block + (3, SIDE, width, lanes), jnp.bfloat16),
            pltpu.VMEM(block + (SIDE + 1, width, lanes), jnp.bfloat16),
            pltpu.VMEM(block + (SIDE + 1, width, lanes), jnp.bfloat16),
            pltpu.VMEM(block + (width, lanes), jnp.bfloat16),
            pltpu.VMEM((GROUPS, 2, width, lanes), jnp.bfloat16),
            pltpu.VMEM((width, 128), jnp.bfloat16),
            pltpu.VMEM((SIDE, SIDE, width, 128), jnp.bfloat16),
            pltpu.VMEM((STOPS, GROUPS, 1, 2 * lanes), jnp.float32),
            pltpu.VMEM((D, D), jnp.bfloat16),
            pltpu.VMEM((D, D), jnp.bfloat16),
            pltpu.VMEM((D, D), jnp.bfloat16),
            pltpu.VMEM((3, D, D), jnp.bfloat16),
            pltpu.SemaphoreType.DMA((4, STOPS, GROUPS)),
            pltpu.SemaphoreType.DMA((4, STOPS, GROUPS)),
            pltpu.SemaphoreType.DMA((GROUPS,)),
            pltpu.SemaphoreType.DMA((GROUPS,)),
            pltpu.SemaphoreType.DMA((2,)),
            pltpu.SemaphoreType.DMA((2,)),
            pltpu.SemaphoreType.DMA((3,)),
        ],
        compiler_params=pltpu.CompilerParams(
            collective_id=0, has_side_effects=True, vmem_limit_bytes=56 << 20
        ),
    )(
        tokens[0].T, norm_gain, expert_ids[0].transpose(0, 2, 1), gate_logits[0].transpose(0, 2, 1),
        w_gate[0], w_up[0], w_down[0],
    )
    return out.T[None]


def solution(mesh):
    placed = (
        P("section", "dp", "expert"),
        P("section", "expert"),
        P("section", None, "expert"),
        P("section", None, "expert"),
        P("section", "expert", None),
        P("section", None, "dp", None),
        P("section", None, "dp", None),
    )
    return jax.shard_map(
        per_device,
        mesh=mesh,
        in_specs=placed,
        out_specs=P("section", "dp", "expert"),
        check_vma=False,
    )
```

time: 144 us -> 105 us (0.73)
  Pallas kernels: 137 us -> 104 us
  local copies, waits for them, and re-layouts: 4.58 us -> 1.54 us
  other arithmetic: 1.53 us -> 0 us
    pallas_call x1, Pallas kernels: 137 us -> 104 us  [per_device(): pl.pallas_call(kernel, out_shape=jax.ShapeDtypeStruct((width, rows), jnp....]
    another operation x2 -> x0, local copies, waits for them, and re-layouts: 1.59 us -> none  [per_device(): split = tokens[0].reshape(GROUPS, 2, lanes, width).transpose(0, 1, 3, 2)]
    unnamed x0 -> x1, local copies, waits for them, and re-layouts: none -> 1.54 us
    add x1 -> x0, other arithmetic: 1.53 us -> none  [per_device(): jnp.where(ids[..., 0] == expert, weight_one, 0.0)]
where the time goes in v2:
time: 105 us
  Pallas kernels  104 us (99%)
  local copies, waits for them, and re-layouts  1.54 us (1%)
    pallas_call x1, Pallas kernels, per_device(): pl.pallas_call(kernel, out_shape=jax.ShapeDtypeStruct((width, rows), jnp....  104 us

profile of v2, /device:TPU:1, one launch (start us, length us, event | category | flops | bytes accessed | tf_op | source)
XLA Modules:
  0.0 105.1 jit_solution(2635234881286467673)
XLA Ops:
  0.0 103.5 %shard_map.73 = bf16[48,1024]{1,0:T(8,128)(2,1)} custom-call(bf16[48,1024]{1,0:T(8,128)(2,1)} %bitcast.19, bf16[1,48]{1,0:T(2,128)(2,1)} %gain_ref.1, s32[4,2,1024]{2,1,0:T(2,128)} %bitcast.20, f32[4,2,1024]{2,1,0:T(2,128)} %bitcast.21, bf16[768,768]{1,0:T(8,128)(2,1)} %bitcast.15, bf16[768,768]{1,0:T(8,128)(2,1)} %bitcast.16, bf16[768,768]{1,0:T(8,128)(2,1)} %bitcast.17), custom_call_target="tpu_custom_call" | custom-call | tf_op jit(solution)/shard_map/pallas_call | solution.py:256
  103.6 1.5 %copy.9 = bf16[1,1024,48]{1,2,0:T(8,128)(2,1)} copy(bf16[1,1024,48]{1,2,0:T(8,128)(2,1)} %bitcast.18) | data formatting | bytes 196608

commit v3 on v2

--- a/solution.py
+++ b/solution.py
@@ -15,11 +15,11 @@
 
 
 def kernel(
-    tokens_ref, gain_ref, ids_ref, logits_ref, gate_ref, up_ref, down_ref,
+    tokens_ref, gain_in, ids_in, logits_in, gate_ref, up_ref, down_ref,
     out_ref,
     gathered, partial, returned, summed, last, held, final, gain_own, gain_all, weight,
-    gate_t, up_t, down_t, raw,
-    recv_sem, send_sem, final_recv, final_send, gain_recv, gain_send, load_sem,
+    gate_t, up_t, down_t, raw, gain_ref, ids_ref, logits_ref,
+    recv_sem, send_sem, gain_recv, gain_send, load_sem, out_sem,
 ):
     section = lax.axis_index("section")
     chip = lax.axis_index("expert")
@@ -42,11 +42,15 @@
     for partner in partners:
         pl.semaphore_signal(barrier, inc=1, device_id=partner, device_id_type=MESH)
     loads = [
-        pltpu.make_async_copy(source, raw.at[i], load_sem.at[i])
-        for i, source in enumerate((gate_ref, up_ref, down_ref))
+        pltpu.make_async_copy(source, target, load_sem.at[i])
+        for i, (source, target) in enumerate((
+            (gain_in, gain_ref), (ids_in, ids_ref), (logits_in, logits_ref),
+            (gate_ref, raw.at[0]), (up_ref, raw.at[1]), (down_ref, raw.at[2]),
+        ))
     ]
     for load in loads:
         load.start()
+    loads[0].wait()
     gain_row = jnp.broadcast_to(gain_ref[...].astype(jnp.float32), (128, SLICE))
     gain_own[...] = gain_row.T.astype(jnp.bfloat16)
     pl.semaphore_wait(barrier, len(partners))
@@ -69,7 +73,7 @@
         return (across, on_line) if half == 0 else (on_line, across)
 
     mine = [(x, y), (y, x)]
-    line_peers = [x_peers, y_peers]
+    line_peers = [[peers[1], peers[0], peers[2]] for peers in (x_peers, y_peers)]
     before = [lax.rem(place[1] + SIDE - 1, SIDE) for place in mine]
     after = [lax.rem(place[1] + 1, SIDE) for place in mine]
     opposite = [lax.rem(place[1] + 2, SIDE) for place in mine]
@@ -86,11 +90,11 @@
 
     def first_step(source, t, g, half, core):
         target = gathered.at[t, g, half, y, x]
-        to_recv, to_send = recv_sem.at[0, t, g], send_sem.at[0, t, g]
+        to_recv, to_send = recv_sem.at[0, t, g], send_sem.at[0]
         on_line, across = mine[half]
+        send(source, target, to_send, to_recv, to_chip(core, half, on_line, opposite[half]))
         for peer in line_peers[half]:
             send(source, target, to_send, to_recv, to_chip(core, half, peer, across))
-        send(source, target, to_send, to_recv, to_chip(core, half, on_line, opposite[half]))
 
     for group in range(GROUPS):
         for half in range(2):
@@ -103,6 +107,8 @@
                 send(gain_own, gain_all.at[y, x], gain_send.at[0], gain_recv.at[0], device(section, peer, x))
 
     expert = chip // 2
+    loads[1].wait()
+    loads[2].wait()
     for t in range(STOPS):
         for g in range(GROUPS):
             span = pl.ds(2 * g * lanes, 2 * lanes)
@@ -113,17 +119,16 @@
 
     def spread(t, g):
         wait_blocks(recv_sem.at[0, t, g], 10)
-        to_recv, to_send = recv_sem.at[1, t, g], send_sem.at[1, t, g]
-        for half in range(2):
-            on_line, across = mine[half]
-            own_line = line(gathered.at[t, g, half], half, across)
-            for beside in (before[half], after[half]):
-                send(own_line, own_line, to_send, to_recv, to_chip(section, half, on_line, beside))
+        to_recv, to_send = recv_sem.at[1, t, g], send_sem.at[1]
         for half in range(2):
             on_line, across = mine[half]
             far = spot(gathered.at[t, g, half], half, on_line, opposite[half])
             for peer in line_peers[half]:
                 send(far, far, to_send, to_recv, to_chip(section, half, peer, across))
+        for side in (before, after):
+            for half in range(2):
+                own_line = line(gathered.at[t, g, half], half, mine[half][1])
+                send(own_line, own_line, to_send, to_recv, to_chip(section, half, mine[half][0], side[half]))
 
     def compute(t, g):
         wait_blocks(recv_sem.at[1, t, g], 22)
@@ -144,21 +149,21 @@
         outcome = (outcome * weight[t, g]).astype(jnp.bfloat16)
         for half in range(2):
             partial[t, g, half] = outcome[:, half * lanes:(half + 1) * lanes].reshape(SIDE, SIDE, SLICE, lanes)
-        to_recv, to_send = recv_sem.at[2, t, g], send_sem.at[2, t, g]
-        for half in range(2):
-            on_line, across = mine[half]
-            for beside, slot in ((before[half], 1), (after[half], 0)):
-                send(line(partial.at[t, g, half], half, beside), returned.at[t, g, half, slot], to_send, to_recv,
-                     to_chip(section, half, on_line, beside))
+        to_recv, to_send = recv_sem.at[2, t, g], send_sem.at[2]
         for half in range(2):
             on_line, across = mine[half]
             for peer in line_peers[half]:
                 send(spot(partial.at[t, g, half], half, peer, opposite[half]), returned.at[t, g, half, 2, on_line],
                      to_send, to_recv, to_chip(section, half, peer, across))
+        for side, slot in ((before, 1), (after, 0)):
+            for half in range(2):
+                send(line(partial.at[t, g, half], half, side[half]), returned.at[t, g, half, slot], to_send, to_recv,
+                     to_chip(section, half, mine[half][0], side[half]))
 
     def collect(t, g):
         wait_blocks(recv_sem.at[2, t, g], 22)
-        to_recv, to_send = recv_sem.at[3, t, g], send_sem.at[3, t, g]
+        core = lax.rem(section + t // (STOPS - 1), 2)
+        to_recv, to_send = recv_sem.at[3, t, g], send_sem.at[3]
         for half in range(2):
             on_line, across = mine[half]
             total = line(partial.at[t, g, half], half, across)[...].astype(jnp.float32)
@@ -170,32 +175,44 @@
             summed[t, g, half, SIDE] = total.astype(jnp.bfloat16)
             for peer in line_peers[half]:
                 send(summed.at[t, g, half, peer], last.at[t, g, half, on_line], to_send, to_recv,
-                     to_chip(section, half, peer, across))
+                     to_chip(core, half, peer, across))
             send(summed.at[t, g, half, SIDE], last.at[t, g, half, SIDE], to_send, to_recv,
-                 to_chip(section, half, on_line, opposite[half]))
+                 to_chip(core, half, on_line, opposite[half]))
+
+            @pl.when(t == STOPS - 1)
+            def _(half=half, on_line=on_line):
+                send(summed.at[t, g, half, on_line], last.at[t, g, half, on_line], to_send, to_recv, device(other, y, x))
+                send(gathered.at[t, g, half, y, x], final.at[g, half], to_send, to_recv, device(other, y, x))
 
     def finish(t, g):
-        wait_blocks(recv_sem.at[3, t, g], 8)
-        for half in range(2):
-            on_line, across = mine[half]
-            total = summed[t, g, half, on_line].astype(jnp.float32) + last[t, g, half, SIDE].astype(jnp.float32)
-            for peer in line_peers[half]:
-                total = total + last[t, g, half, peer].astype(jnp.float32)
-            total = gathered[t, g, half, y, x].astype(jnp.float32) + total
-            held[t, g, half] = total.astype(jnp.bfloat16)
-
         @pl.when(t < STOPS - 1)
         def _():
+            wait_blocks(recv_sem.at[3, t, g], 8)
             later = jnp.minimum(t + 1, STOPS - 1)
             for half in range(2):
+                on_line, across = mine[half]
+                total = summed[t, g, half, on_line].astype(jnp.float32) + last[t, g, half, SIDE].astype(jnp.float32)
+                for peer in line_peers[half]:
+                    total = total + last[t, g, half, peer].astype(jnp.float32)
+                total = gathered[t, g, half, y, x].astype(jnp.float32) + total
+                held[t, g, half] = total.astype(jnp.bfloat16)
                 block = held.at[t, g, half]
                 first_step(block, later, g, half, other)
-                send(block, gathered.at[later, g, half, y, x], send_sem.at[0, later, g], recv_sem.at[0, later, g],
+                send(block, gathered.at[later, g, half, y, x], send_sem.at[0], recv_sem.at[0, later, g],
                      device(other, y, x))
 
         @pl.when(t == STOPS - 1)
         def _():
-            send(held.at[t, g], final.at[g], final_send.at[g], final_recv.at[g], device(other, y, x))
+            wait_blocks(recv_sem.at[3, t, g], 12)
+            for half in range(2):
+                total = jnp.sum(last[t, g, half].astype(jnp.float32), axis=0)
+                total = final[g, half].astype(jnp.float32) + total
+                held[t, g, half] = total.astype(jnp.bfloat16)
+                to_out(t, g, half).start()
+
+    def to_out(t, g, half):
+        span = pl.ds(pl.multiple_of((2 * g + half) * lanes, lanes), lanes)
+        return pltpu.make_async_copy(held.at[t, g, half], out_ref.at[:, span], out_sem.at[g, half])
 
     def each_group(stage, t):
         def one(g, carry):
@@ -208,7 +225,7 @@
     for peer in x_peers:
         send(gain_all.at[:, x], gain_all.at[:, x], gain_send.at[1], gain_recv.at[1], device(section, y, peer))
     for i, target in enumerate((gate_t, up_t, down_t)):
-        loads[i].wait()
+        loads[i + 3].wait()
         target[...] = raw[i].T
     wait_gain(gain_recv.at[1], 12)
 
@@ -224,40 +241,28 @@
 
     lax.fori_loop(0, STOPS, stop, 0)
 
-    def settle(t, carry):
-        for g in range(GROUPS):
-            for k, blocks in ((1, 22), (2, 22), (3, 8)):
-                wait_blocks(send_sem.at[k, t, g], blocks)
-
-            @pl.when(t == 0)
-            def _():
-                wait_blocks(send_sem.at[0, 0, g], 8)
-
-            @pl.when(t > 0)
-            def _():
-                wait_blocks(send_sem.at[0, t, g], 10)
-        return carry
-
-    lax.fori_loop(0, STOPS, settle, 0)
+    steps = STOPS * GROUPS
+    sent = (8 * GROUPS + 10 * (steps - GROUPS), 22 * steps, 22 * steps, 8 * (steps - GROUPS) + 12 * GROUPS)
+    for k, blocks in enumerate(sent):
+        view = gathered.reshape(steps * 2 * SIDE * SIDE, SLICE, lanes).at[pl.ds(0, blocks)]
+        pltpu.make_async_copy(view, view, send_sem.at[k]).wait()
     wait_gain(gain_send.at[0], 3)
     wait_gain(gain_send.at[1], 12)
     for g in range(GROUPS):
-        wait_blocks(final_send.at[g], 2)
-        wait_blocks(final_recv.at[g], 2)
-        for half in range(2):
-            out_ref[:, (2 * g + half) * lanes:(2 * g + half + 1) * lanes] = final[g, half]
+        for half in range(2):
+            to_out(STOPS - 1, g, half).wait()
 
 
 def per_device(tokens, norm_gain, w_gate, w_up, w_down, expert_ids, gate_logits):
     rows, width = tokens.shape[1:]
     lanes = rows // (2 * GROUPS)
     block = (STOPS, GROUPS, 2)
-    vmem = pl.BlockSpec(memory_space=pltpu.VMEM)
+    anywhere = pl.BlockSpec(memory_space=pl.ANY)
     out = pl.pallas_call(
         kernel,
         out_shape=jax.ShapeDtypeStruct((width, rows), jnp.bfloat16),
-        in_specs=[vmem] * 4 + [pl.BlockSpec(memory_space=pl.ANY)] * 3,
-        out_specs=vmem,
+        in_specs=[anywhere] * 7,
+        out_specs=anywhere,
         scratch_shapes=[
             pltpu.VMEM(block + (SIDE, SIDE, width, lanes), jnp.bfloat16),
             pltpu.VMEM(block + (SIDE, SIDE, width, lanes), jnp.bfloat16),
@@ -273,13 +278,15 @@
             pltpu.VMEM((D, D), jnp.bfloat16),
             pltpu.VMEM((D, D), jnp.bfloat16),
             pltpu.VMEM((3, D, D), jnp.bfloat16),
+            pltpu.VMEM((1, width), jnp.bfloat16),
+            pltpu.VMEM((STOPS, 2, rows), jnp.int32),
+            pltpu.VMEM((STOPS, 2, rows), jnp.float32),
             pltpu.SemaphoreType.DMA((4, STOPS, GROUPS)),
-            pltpu.SemaphoreType.DMA((4, STOPS, GROUPS)),
-            pltpu.SemaphoreType.DMA((GROUPS,)),
-            pltpu.SemaphoreType.DMA((GROUPS,)),
+            pltpu.SemaphoreType.DMA((4,)),
             pltpu.SemaphoreType.DMA((2,)),
             pltpu.SemaphoreType.DMA((2,)),
-            pltpu.SemaphoreType.DMA((3,)),
+            pltpu.SemaphoreType.DMA((6,)),
+            pltpu.SemaphoreType.DMA((GROUPS, 2)),
         ],
         compiler_params=pltpu.CompilerParams(
             collective_id=0, has_side_effects=True, vmem_limit_bytes=56 << 20

time: 105 us -> 100 us (0.952)
  Pallas kernels: 104 us -> 98.5 us
    pallas_call x1, Pallas kernels: 104 us -> 98.5 us  [per_device(): pl.pallas_call(kernel, out_shape=jax.ShapeDtypeStruct((width, rows), jnp....]
where the time goes in v3:
time: 100 us
  Pallas kernels  98.5 us (98%)
  local copies, waits for them, and re-layouts  1.54 us (2%)
    pallas_call x1, Pallas kernels, per_device(): pl.pallas_call(kernel, out_shape=jax.ShapeDtypeStruct((width, rows), jnp....  98.5 us

profile of v3, /device:TPU:1, one launch (start us, length us, event | category | flops | bytes accessed | tf_op | source)
XLA Modules:
  0.0 100.0 jit_solution(871280358818474793)
XLA Ops:
  0.0 98.5 %shard_map.73 = bf16[48,1024]{1,0:T(8,128)(2,1)} custom-call(bf16[48,1024]{1,0:T(8,128)(2,1)} %bitcast.19, bf16[1,48]{1,0:T(2,128)(2,1)} %gain_in.1, s32[4,2,1024]{2,1,0:T(2,128)} %bitcast.20, f32[4,2,1024]{2,1,0:T(2,128)} %bitcast.21, bf16[768,768]{1,0:T(8,128)(2,1)} %bitcast.15, bf16[768,768]{1,0:T(8,128)(2,1)} %bitcast.16, bf16[768,768]{1,0:T(8,128)(2,1)} %bitcast.17), custom_call_target="tpu_custom_call" | custom-call | tf_op jit(solution)/shard_map/pallas_call | solution.py:261
  98.5 1.5 %copy.9 = bf16[1,1024,48]{1,2,0:T(8,128)(2,1)} copy(bf16[1,1024,48]{1,2,0:T(8,128)(2,1)} %bitcast.18) | data formatting | bytes 196608

commit v4 on v3

--- a/solution.py
+++ b/solution.py
@@ -95,6 +95,8 @@
         send(source, target, to_send, to_recv, to_chip(core, half, on_line, opposite[half]))
         for peer in line_peers[half]:
             send(source, target, to_send, to_recv, to_chip(core, half, peer, across))
+        for side in (before, after):
+            send(source, target, to_send, to_recv, to_chip(core, half, on_line, side[half]))
 
     for group in range(GROUPS):
         for half in range(2):
@@ -118,7 +120,7 @@
             weight[t, g] = jnp.where(ids[0:1] == expert, one, 0.0) + jnp.where(ids[1:2] == expert, two, 0.0)
 
     def spread(t, g):
-        wait_blocks(recv_sem.at[0, t, g], 10)
+        wait_blocks(recv_sem.at[0, t, g], 14)
         to_recv, to_send = recv_sem.at[1, t, g], send_sem.at[1]
         for half in range(2):
             on_line, across = mine[half]
@@ -127,11 +129,13 @@
                 send(far, far, to_send, to_recv, to_chip(section, half, peer, across))
         for side in (before, after):
             for half in range(2):
-                own_line = line(gathered.at[t, g, half], half, mine[half][1])
-                send(own_line, own_line, to_send, to_recv, to_chip(section, half, mine[half][0], side[half]))
+                on_line, across = mine[half]
+                for peer in line_peers[half]:
+                    block = spot(gathered.at[t, g, half], half, peer, across)
+                    send(block, block, to_send, to_recv, to_chip(section, half, on_line, side[half]))
 
     def compute(t, g):
-        wait_blocks(recv_sem.at[1, t, g], 22)
+        wait_blocks(recv_sem.at[1, t, g], 18)
         acts = jnp.concatenate(
             [gathered[t, g, half].reshape(D, lanes) for half in range(2)], axis=1
         ).astype(jnp.float32)
@@ -157,42 +161,48 @@
                      to_send, to_recv, to_chip(section, half, peer, across))
         for side, slot in ((before, 1), (after, 0)):
             for half in range(2):
-                send(line(partial.at[t, g, half], half, side[half]), returned.at[t, g, half, slot], to_send, to_recv,
-                     to_chip(section, half, mine[half][0], side[half]))
+                on_line, across = mine[half]
+                for peer in line_peers[half]:
+                    send(spot(partial.at[t, g, half], half, peer, side[half]), returned.at[t, g, half, slot, peer],
+                         to_send, to_recv, to_chip(section, half, on_line, side[half]))
 
     def collect(t, g):
-        wait_blocks(recv_sem.at[2, t, g], 22)
+        wait_blocks(recv_sem.at[2, t, g], 18)
         core = lax.rem(section + t // (STOPS - 1), 2)
         to_recv, to_send = recv_sem.at[3, t, g], send_sem.at[3]
         for half in range(2):
             on_line, across = mine[half]
-            total = line(partial.at[t, g, half], half, across)[...].astype(jnp.float32)
-            total = total + returned[t, g, half, 0].astype(jnp.float32) + returned[t, g, half, 1].astype(jnp.float32)
-            summed[t, g, half, 0:SIDE] = total.astype(jnp.bfloat16)
             total = spot(partial.at[t, g, half], half, on_line, opposite[half])[...].astype(jnp.float32)
             for peer in line_peers[half]:
                 total = total + returned[t, g, half, 2, peer].astype(jnp.float32)
             summed[t, g, half, SIDE] = total.astype(jnp.bfloat16)
+            send(summed.at[t, g, half, SIDE], last.at[t, g, half, SIDE], to_send, to_recv,
+                 to_chip(core, half, on_line, opposite[half]))
             for peer in line_peers[half]:
+                total = spot(partial.at[t, g, half], half, peer, across)[...].astype(jnp.float32)
+                for slot in range(2):
+                    total = total + returned[t, g, half, slot, peer].astype(jnp.float32)
+                summed[t, g, half, peer] = total.astype(jnp.bfloat16)
                 send(summed.at[t, g, half, peer], last.at[t, g, half, on_line], to_send, to_recv,
                      to_chip(core, half, peer, across))
-            send(summed.at[t, g, half, SIDE], last.at[t, g, half, SIDE], to_send, to_recv,
-                 to_chip(core, half, on_line, opposite[half]))
+            for side, slot in ((before, SIDE + 2), (after, SIDE + 1)):
+                send(spot(partial.at[t, g, half], half, on_line, side[half]), last.at[t, g, half, slot], to_send, to_recv,
+                     to_chip(core, half, on_line, side[half]))
 
             @pl.when(t == STOPS - 1)
             def _(half=half, on_line=on_line):
-                send(summed.at[t, g, half, on_line], last.at[t, g, half, on_line], to_send, to_recv, device(other, y, x))
+                send(partial.at[t, g, half, y, x], last.at[t, g, half, on_line], to_send, to_recv, device(other, y, x))
                 send(gathered.at[t, g, half, y, x], final.at[g, half], to_send, to_recv, device(other, y, x))
 
     def finish(t, g):
         @pl.when(t < STOPS - 1)
         def _():
-            wait_blocks(recv_sem.at[3, t, g], 8)
+            wait_blocks(recv_sem.at[3, t, g], 12)
             later = jnp.minimum(t + 1, STOPS - 1)
             for half in range(2):
                 on_line, across = mine[half]
-                total = summed[t, g, half, on_line].astype(jnp.float32) + last[t, g, half, SIDE].astype(jnp.float32)
-                for peer in line_peers[half]:
+                total = partial[t, g, half, y, x].astype(jnp.float32)
+                for peer in line_peers[half] + [SIDE, SIDE + 1, SIDE + 2]:
                     total = total + last[t, g, half, peer].astype(jnp.float32)
                 total = gathered[t, g, half, y, x].astype(jnp.float32) + total
                 held[t, g, half] = total.astype(jnp.bfloat16)
@@ -203,7 +213,7 @@
 
         @pl.when(t == STOPS - 1)
         def _():
-            wait_blocks(recv_sem.at[3, t, g], 12)
+            wait_blocks(recv_sem.at[3, t, g], 16)
             for half in range(2):
                 total = jnp.sum(last[t, g, half].astype(jnp.float32), axis=0)
                 total = final[g, half].astype(jnp.float32) + total
@@ -220,10 +230,12 @@
             return carry
         lax.fori_loop(0, GROUPS, one, 0)
 
-    each_group(spread, 0)
-    wait_gain(gain_recv.at[0], 4)
-    for peer in x_peers:
-        send(gain_all.at[:, x], gain_all.at[:, x], gain_send.at[1], gain_recv.at[1], device(section, y, peer))
+    for g in range(GROUPS):
+        spread(0, g)
+        if g == 0:
+            wait_gain(gain_recv.at[0], 4)
+            for peer in x_peers:
+                send(gain_all.at[:, x], gain_all.at[:, x], gain_send.at[1], gain_recv.at[1], device(section, y, peer))
     for i, target in enumerate((gate_t, up_t, down_t)):
         loads[i + 3].wait()
         target[...] = raw[i].T
@@ -242,7 +254,7 @@
     lax.fori_loop(0, STOPS, stop, 0)
 
     steps = STOPS * GROUPS
-    sent = (8 * GROUPS + 10 * (steps - GROUPS), 22 * steps, 22 * steps, 8 * (steps - GROUPS) + 12 * GROUPS)
+    sent = (12 * GROUPS + 14 * (steps - GROUPS), 18 * steps, 18 * steps, 12 * (steps - GROUPS) + 16 * GROUPS)
     for k, blocks in enumerate(sent):
         view = gathered.reshape(steps * 2 * SIDE * SIDE, SLICE, lanes).at[pl.ds(0, blocks)]
         pltpu.make_async_copy(view, view, send_sem.at[k]).wait()
@@ -268,7 +280,7 @@
             pltpu.VMEM(block + (SIDE, SIDE, width, lanes), jnp.bfloat16),
             pltpu.VMEM(block + (3, SIDE, width, lanes), jnp.bfloat16),
             pltpu.VMEM(block + (SIDE + 1, width, lanes), jnp.bfloat16),
-            pltpu.VMEM(block + (SIDE + 1, width, lanes), jnp.bfloat16),
+            pltpu.VMEM(block + (SIDE + 3, width, lanes), jnp.bfloat16),
             pltpu.VMEM(block + (width, lanes), jnp.bfloat16),
             pltpu.VMEM((GROUPS, 2, width, lanes), jnp.bfloat16),
             pltpu.VMEM((width, 128), jnp.bfloat16),

time: 100 us -> 93.3 us (0.933)
  Pallas kernels: 98.5 us -> 91.7 us
    pallas_call x1, Pallas kernels: 98.5 us -> 91.7 us  [per_device(): pl.pallas_call(kernel, out_shape=jax.ShapeDtypeStruct((width, rows), jnp....]
where the time goes in v4:
time: 93.3 us; the launch traced here: 93.2 us
  Pallas kernels  91.7 us (98%)
  local copies, waits for them, and re-layouts  1.54 us (2%)
    pallas_call x1, Pallas kernels, per_device(): pl.pallas_call(kernel, out_shape=jax.ShapeDtypeStruct((width, rows), jnp....  91.7 us

profile of v4, /device:TPU:1, one launch (start us, length us, event | category | flops | bytes accessed | tf_op | source)
XLA Modules:
  0.0 93.2 jit_solution(16027958059832856490)
XLA Ops:
  0.0 91.7 %shard_map.73 = bf16[48,1024]{1,0:T(8,128)(2,1)} custom-call(bf16[48,1024]{1,0:T(8,128)(2,1)} %bitcast.19, bf16[1,48]{1,0:T(2,128)(2,1)} %gain_in.1, s32[4,2,1024]{2,1,0:T(2,128)} %bitcast.20, f32[4,2,1024]{2,1,0:T(2,128)} %bitcast.21, bf16[768,768]{1,0:T(8,128)(2,1)} %bitcast.15, bf16[768,768]{1,0:T(8,128)(2,1)} %bitcast.16, bf16[768,768]{1,0:T(8,128)(2,1)} %bitcast.17), custom_call_target="tpu_custom_call" | custom-call | tf_op jit(solution)/shard_map/pallas_call | solution.py:273
  91.7 1.5 %copy.9 = bf16[1,1024,48]{1,2,0:T(8,128)(2,1)} copy(bf16[1,1024,48]{1,2,0:T(8,128)(2,1)} %bitcast.18) | data formatting | bytes 196608

commit v5 on v4

--- a/solution.py
+++ b/solution.py
@@ -136,17 +136,16 @@
 
     def compute(t, g):
         wait_blocks(recv_sem.at[1, t, g], 18)
-        acts = jnp.concatenate(
-            [gathered[t, g, half].reshape(D, lanes) for half in range(2)], axis=1
-        ).astype(jnp.float32)
+        acts = jnp.concatenate([gathered[t, g, half].reshape(D, lanes) for half in range(2)], axis=1)
+        gain = gain_all[...].reshape(D, 128)
+        gain = jnp.concatenate([gain] * (2 * lanes // 128), axis=1)
+        acts = acts.astype(jnp.float32)
+        scaled = (acts * gain.astype(jnp.float32)).astype(jnp.bfloat16)
         inverse = lax.rsqrt(jnp.sum(acts * acts, axis=0, keepdims=True) / D + 1e-05)
-        gain = gain_all[...].reshape(D, 128).astype(jnp.float32)
-        gain = jnp.concatenate([gain] * (2 * lanes // 128), axis=1)
-        normed = (acts * inverse * gain).astype(jnp.bfloat16)
         pieces = []
         for start in range(0, D, PIECE):
-            gate_val = jnp.dot(gate_t[start:start + PIECE], normed, preferred_element_type=jnp.float32)
-            up_val = jnp.dot(up_t[start:start + PIECE], normed, preferred_element_type=jnp.float32)
+            gate_val = jnp.dot(gate_t[start:start + PIECE], scaled, preferred_element_type=jnp.float32) * inverse
+            up_val = jnp.dot(up_t[start:start + PIECE], scaled, preferred_element_type=jnp.float32) * inverse
             pieces.append((jax.nn.silu(gate_val) * up_val).astype(jnp.bfloat16))
         hidden = jnp.concatenate(pieces, axis=0)
         outcome = jnp.dot(down_t[...], hidden, preferred_element_type=jnp.float32)
@@ -243,12 +242,15 @@
 
     def stop(t, carry):
         each_group(compute, t)
-        each_group(collect, t)
-        each_group(finish, t)
+        for g in range(GROUPS):
+            collect(t, g)
+        for g in range(GROUPS):
+            finish(t, g)
 
         @pl.when(t < STOPS - 1)
         def _():
-            each_group(spread, jnp.minimum(t + 1, STOPS - 1))
+            for g in range(GROUPS):
+                spread(jnp.minimum(t + 1, STOPS - 1), g)
         return carry
 
     lax.fori_loop(0, STOPS, stop, 0)

time: 93.3 us -> 91.8 us (0.984)
  Pallas kernels: 91.7 us -> 90.1 us
    pallas_call x1, Pallas kernels: 91.7 us -> 90.1 us  [per_device(): pl.pallas_call(kernel, out_shape=jax.ShapeDtypeStruct((width, rows), jnp....]
where the time goes in v5:
time: 91.8 us; the launch traced here: 91.7 us
  Pallas kernels  90.1 us (98%)
  local copies, waits for them, and re-layouts  1.54 us (2%)
    pallas_call x1, Pallas kernels, per_device(): pl.pallas_call(kernel, out_shape=jax.ShapeDtypeStruct((width, rows), jnp....  90.1 us

profile of v5, /device:TPU:1, one launch (start us, length us, event | category | flops | bytes accessed | tf_op | source)
XLA Modules:
  0.0 91.7 jit_solution(1783898642560440785)
XLA Ops:
  0.0 90.1 %shard_map.73 = bf16[48,1024]{1,0:T(8,128)(2,1)} custom-call(bf16[48,1024]{1,0:T(8,128)(2,1)} %bitcast.19, bf16[1,48]{1,0:T(2,128)(2,1)} %gain_in.1, s32[4,2,1024]{2,1,0:T(2,128)} %bitcast.20, f32[4,2,1024]{2,1,0:T(2,128)} %bitcast.21, bf16[768,768]{1,0:T(8,128)(2,1)} %bitcast.15, bf16[768,768]{1,0:T(8,128)(2,1)} %bitcast.16, bf16[768,768]{1,0:T(8,128)(2,1)} %bitcast.17), custom_call_target="tpu_custom_call" | custom-call | tf_op jit(solution)/shard_map/pallas_call | solution.py:275
  90.1 1.5 %copy.9 = bf16[1,1024,48]{1,2,0:T(8,128)(2,1)} copy(bf16[1,1024,48]{1,2,0:T(8,128)(2,1)} %bitcast.18) | data formatting | bytes 196608

commit v6 on v5

--- a/solution.py
+++ b/solution.py
@@ -15,10 +15,10 @@
 
 
 def kernel(
-    tokens_ref, gain_in, ids_in, logits_in, gate_ref, up_ref, down_ref,
+    tokens_in, gain_in, ids_in, logits_in, gate_ref, up_ref, down_ref,
     out_ref,
     gathered, partial, returned, summed, last, held, final, gain_own, gain_all, weight,
-    gate_t, up_t, down_t, raw, gain_ref, ids_ref, logits_ref,
+    gate_t, up_t, down_t, raw, gain_ref, ids_ref, logits_ref, tokens_ref,
     recv_sem, send_sem, gain_recv, gain_send, load_sem, out_sem,
 ):
     section = lax.axis_index("section")
@@ -45,14 +45,15 @@
         pltpu.make_async_copy(source, target, load_sem.at[i])
         for i, (source, target) in enumerate((
             (gain_in, gain_ref), (ids_in, ids_ref), (logits_in, logits_ref),
-            (gate_ref, raw.at[0]), (up_ref, raw.at[1]), (down_ref, raw.at[2]),
+            (gate_ref, raw.at[0]), (up_ref, raw.at[1]), (down_ref, raw.at[2]), (tokens_in, tokens_ref),
         ))
     ]
-    for load in loads:
+    for load in loads[6:] + loads[:3]:
         load.start()
     loads[0].wait()
     gain_row = jnp.broadcast_to(gain_ref[...].astype(jnp.float32), (128, SLICE))
     gain_own[...] = gain_row.T.astype(jnp.bfloat16)
+    loads[6].wait()
     pl.semaphore_wait(barrier, len(partners))
 
     def send(source, target, send_at, recv_at, to):
@@ -107,6 +108,9 @@
             pltpu.make_async_copy(gain_own, gain_all.at[y, x], gain_recv.at[0]).start()
             for peer in y_peers:
                 send(gain_own, gain_all.at[y, x], gain_send.at[0], gain_recv.at[0], device(section, peer, x))
+
+    for load in loads[3:6]:
+        load.start()
 
     expert = chip // 2
     loads[1].wait()
@@ -295,11 +299,12 @@
             pltpu.VMEM((1, width), jnp.bfloat16),
             pltpu.VMEM((STOPS, 2, rows), jnp.int32),
             pltpu.VMEM((STOPS, 2, rows), jnp.float32),
+            pltpu.VMEM((width, rows), jnp.bfloat16),
             pltpu.SemaphoreType.DMA((4, STOPS, GROUPS)),
             pltpu.SemaphoreType.DMA((4,)),
             pltpu.SemaphoreType.DMA((2,)),
             pltpu.SemaphoreType.DMA((2,)),
-            pltpu.SemaphoreType.DMA((6,)),
+            pltpu.SemaphoreType.DMA((7,)),
             pltpu.SemaphoreType.DMA((GROUPS, 2)),
         ],
         compiler_params=pltpu.CompilerParams(

time: 91.8 us -> 91.6 us (level)
  no operation moved by 1% of the time
where the time goes in v6:
time: 91.6 us; the launch traced here: 91.4 us
  Pallas kernels  89.9 us (98%)
  local copies, waits for them, and re-layouts  1.54 us (2%)
    pallas_call x1, Pallas kernels, per_device(): pl.pallas_call(kernel, out_shape=jax.ShapeDtypeStruct((width, rows), jnp....  89.9 us

profile of v6, /device:TPU:1, one launch (start us, length us, event | category | flops | bytes accessed | tf_op | source)
XLA Modules:
  0.0 91.4 jit_solution(15946460191174551085)
XLA Ops:
  0.0 89.9 %shard_map.73 = bf16[48,1024]{1,0:T(8,128)(2,1)} custom-call(bf16[48,1024]{1,0:T(8,128)(2,1)} %bitcast.19, bf16[1,48]{1,0:T(2,128)(2,1)} %gain_in.1, s32[4,2,1024]{2,1,0:T(2,128)} %bitcast.20, f32[4,2,1024]{2,1,0:T(2,128)} %bitcast.21, bf16[768,768]{1,0:T(8,128)(2,1)} %bitcast.15, bf16[768,768]{1,0:T(8,128)(2,1)} %bitcast.16, bf16[768,768]{1,0:T(8,128)(2,1)} %bitcast.17), custom_call_target="tpu_custom_call" | custom-call | tf_op jit(solution)/shard_map/pallas_call | solution.py:279
  89.9 1.5 %copy.9 = bf16[1,1024,48]{1,2,0:T(8,128)(2,1)} copy(bf16[1,1024,48]{1,2,0:T(8,128)(2,1)} %bitcast.18) | data formatting | bytes 196608
